TPU v7x, 256 devices: a whole 4x4x8 slice. The times are simulated.
256 devices in a mesh: dp: 4 (over x), shard: 64 (over y, z, core).
Axes of the slice: x: 4, y: 4, z: 8, core: 2. Of those that a mesh axis runs over, the one named last changes fastest.
Arguments:
- partial_grads: float32 [4, 112, 768, 1024], P('dp', None, 'shard'), may hold values from -60 to 60
- momentum: float32 [112, 768, 1024], P('dp', 'shard'), may hold values from -6 to 6
- owners: int32 [112], replicated, may hold values from 0 to 63, as said below
Outputs:
- new_momentum: float32 [112, 768, 1024], P('dp', 'shard')
- update: float32 [112, 768, 1024], P('dp', 'shard')
- owned: bfloat16 [4, 64, 768, 1024], P('dp', 'shard')
Inputs may be any that keep to these rules, and one draw needn't show every extreme that they name: Entries 28 * p to 28 * (p + 1) - 1 name the owners of the matrices that the p-th index of dp holds after the sum. No owner gets more than 1 matrices of one group, and in every group some owner gets exactly 1.
All inputs are finite; a program needn't handle non-finite values.
Results may differ from a plain program's by a relative error of at most 0.014.
Values may be sent and summed in bfloat16 or wider, within the bound.
A program may use at most 64 MiB of HBM per device.

v0:
```python
import math

import jax
import jax.numpy as jnp
from jax import lax
from jax.sharding import PartitionSpec as P

D = 1024
F = 768
ITERS = 2


momentum_decay = 0.95
epsilon_norm = 1e-07
coeff_first = 3.4445
coeff_second = -4.775
coeff_third = 2.0315


def orthogonalize(matrices):
    widened = matrices.astype(jnp.float32)
    frobenius = jnp.sqrt(jnp.sum(widened * widened, axis=(1, 2), keepdims=True))
    iterate = (widened / (frobenius + epsilon_norm)).astype(jnp.bfloat16)
    for sweep in range(ITERS):
        gram_matrix = jnp.einsum(
            "kfd,kgd->kfg", iterate, iterate, preferred_element_type=jnp.float32
        ).astype(jnp.bfloat16)
        gram_square = jnp.einsum(
            "kfg,kgh->kfh", gram_matrix, gram_matrix, preferred_element_type=jnp.float32
        )
        poly_term = (
            coeff_second * gram_matrix.astype(jnp.float32) + coeff_third * gram_square
        ).astype(jnp.bfloat16)
        product = jnp.einsum("kfg,kgd->kfd", poly_term, iterate, preferred_element_type=jnp.float32)
        iterate = (coeff_first * iterate.astype(jnp.float32) + product).astype(jnp.bfloat16)
    return iterate


def send_back(orthogonal):
    return lax.all_to_all(orthogonal[None], "shard", split_axis=2, concat_axis=0, tiled=True)


def local(partial_grads, momentum, owners):
    gradient = lax.psum_scatter(partial_grads[0], "dp", scatter_dimension=0, tiled=True)
    new_momentum = momentum_decay * momentum + gradient
    nesterov = (gradient + momentum_decay * new_momentum).astype(jnp.bfloat16)
    task_count = nesterov.shape[0]
    block_rows = nesterov.shape[1]
    columns = nesterov.shape[2]
    owner_count = lax.axis_size("shard")
    group_index = lax.axis_index("dp")
    task_index = jnp.arange(task_count, dtype=jnp.int32)
    slot_count = -(-task_count // owner_count)
    owner_of = lax.dynamic_slice_in_dim(owners, group_index * task_count, task_count)
    earlier_same = (owner_of[:, None] == owner_of[None, :]) & (
        task_index[None, :] < task_index[:, None]
    )
    slot_of = jnp.sum(earlier_same.astype(jnp.int32), axis=1)
    target_slot = owner_of * slot_count + slot_of
    route_table = (
        jnp.arange(owner_count * slot_count, dtype=jnp.int32)[:, None] == target_slot[None, :]
    ).astype(jnp.bfloat16)
    flattened = nesterov.reshape(task_count, block_rows * columns)
    outgoing = jnp.dot(route_table, flattened, preferred_element_type=jnp.float32).astype(
        jnp.bfloat16
    )
    outgoing = outgoing.reshape(owner_count, slot_count, block_rows, columns)
    finished = orthogonalize(
        lax.all_to_all(outgoing, "shard", split_axis=0, concat_axis=2, tiled=True)[0]
    )
    returned_rows = send_back(finished)
    owned = finished[None]
    collected = jnp.dot(
        route_table.T,
        returned_rows.reshape(owner_count * slot_count, block_rows * columns),
        preferred_element_type=jnp.float32,
    )
    update = (collected * (0.2 * math.sqrt(max(F, D)))).reshape(task_count, block_rows, columns)
    return (new_momentum, update, owned)


def solution(mesh):
    return jax.shard_map(
        local,
        mesh=mesh,
        in_specs=(P("dp", None, "shard", None), P("dp", "shard", None), P()),
        out_specs=(P("dp", "shard", None), P("dp", "shard", None), P("dp", "shard", None, None)),
        check_vma=False,
    )
```

profile of v0, /device:TPU:1, one launch (start us, length us, event | category | flops | bytes accessed | tf_op | source)
XLA Modules:
  0.0 319.6 jit_solution(16729561032985313572)
XLA Ops:
  7.2 0.0 all-reduce.3.cloned.1.call-start
  7.2 0.0 copy-start.2
  7.2 0.0 copy-start.1
  7.2 0.0 copy-start
  7.2 0.6 all-reduce.3.cloned.1.call-update
  7.9 0.0 copy-done.2
  7.9 0.6 dynamic-slice
  9.2 0.0 copy-done.1
  9.2 0.1 dynamic_slice.3
  9.2 0.2 convert_reduce_fusion
  9.4 0.1 dynamic-slice_add_fusion
  9.5 123.9 %all-reduce.3.cloned.1.call-done = f32[112,12,1024]{2,0,1:T(8,128)} async-done(((f32[112,12,1024]{2,0,1:T(8,128)}), f32[112,12,1024]{2,0,1:T(8,128)}) %all-reduce.3.cloned.1.call-update) | async-done | bytes 5505040
  133.4 0.0 copy-done
  133.4 3.1 add_convert_fusion.4
  136.5 0.4 copy.17
  136.9 0.1 pad
  137.0 0.4 copy.23
  137.5 0.6 convolution_convert_fusion
  138.1 2.2 reshape.113
  140.2 62.0 %all_to_all.8 = bf16[64,1,12,1024]{3,2,1,0:T(8,128)(2,1)S(1)} all-to-all(bf16[64,1,12,1024]{3,2,1,0:T(8,128)(2,1)} %bitcast.28), channel_id=1, replica_groups=mesh['dp'=4,'shard'=64] {'shard'}, dimensions={0} | all-to-all | bytes 3145728 | tf_op jit(solution)/shard_map/all_to_all | solution.py:69
  202.2 1.7 fusion
  204.6 1.9 fusion.1
  206.5 2.7 convert_element_type.95
  209.2 2.4 convolution_convert_fusion.2
  211.6 4.6 %add_convert_fusion.1 = bf16[768,1024]{1,0:T(8,128)(2,1)S(1)} fusion(bf16[768,1024]{1,0:T(8,128)(2,1)S(1)} %convert_element_type.95, bf16[768,768]{1,0:T(8,128)(2,1)} %convolution_convert_fusion.2), kind=kOutput, calls=%fused_computation.7 | convolution fusion | flops 2120024064 | bytes 4325376 | tf_op jit(solution)/shard_map/kfg,kgd->kfd/dot_general | solution.py:34
  216.2 1.4 convolution_convert_fusion.1
  217.7 3.5 %fusion.2 = bf16[1,1,768,1024]{3,2,1,0:T(8,128)(2,1)} fusion(bf16[768,1024]{1,0:T(8,128)(2,1)S(1)} %add_convert_fusion.1, bf16[768,768]{1,0:T(8,128)(2,1)S(1)} %convolution_convert_fusion.1), kind=kOutput, calls=%fused_computation.14 | convolution fusion | flops 2120024064 | bytes 4325376 | tf_op jit(solution)/shard_map/kfg,kgd->kfd/dot_general | solution.py:34
  221.1 3.8 %copy.25 = bf16[1,1,768,1024]{3,1,0,2:T(2,128)(2,1)S(1)} copy(bf16[1,1,768,1024]{3,2,1,0:T(8,128)(2,1)} %fusion.2) | data formatting | bytes 3145728 | tf_op jit(solution)/shard_map/broadcast_in_dim | solution.py:40
  225.0 0.6 broadcast.61
  225.6 11.3 %reduce.4 = bf16[768,1024]{1,0:T(8,128)(2,1)} reduce(bf16[768,1,1,1024]{3,2,1,0:T(2,128)(2,1)S(1)} %bitcast.27, bf16[]{:T(256)} %broadcast.61), dimensions={1,2}, to_apply=%bitcast.26.reduce_sub_computation | reduce | bytes 3145730
  236.8 3.9 %reshape.120 = bf16[64,2,6144]{2,1,0:T(2,128)(2,1)S(1)} reshape(bf16[768,1024]{1,0:T(8,128)(2,1)} %reduce.4) | data formatting | bytes 3145728
  240.7 45.7 %all_to_all.9 = bf16[64,2,6144]{2,1,0:T(2,128)(2,1)} all-to-all(bf16[64,2,6144]{2,1,0:T(2,128)(2,1)S(1)} %reshape.120), channel_id=1, replica_groups=mesh['dp'=4,'shard'=64] {'shard'}, dimensions={0} | all-to-all | bytes 3145728 | tf_op jit(solution)/shard_map/all_to_all | solution.py:40
  286.5 9.1 %reshape.121 = bf16[768,1,1,1024]{3,2,1,0:T(2,128)(2,1)S(1)} reshape(bf16[64,2,6144]{2,1,0:T(2,128)(2,1)} %all_to_all.9) | data formatting | bytes 3145728
  295.6 10.4 %bitcast_reduce_fusion = bf16[768,1024]{1,0:T(8,128)(2,1)} fusion(bf16[768,1,1,1024]{3,2,1,0:T(2,128)(2,1)S(1)} %reshape.121), kind=kLoop, calls=%fused_computation.25 | loop fusion | bytes 3145728 | tf_op jit(solution)/shard_map/all_to_all | solution.py:40
  306.0 3.5 %reshape.114 = bf16[64,12288]{1,0:T(8,128)(2,1)S(1)} reshape(bf16[768,1024]{1,0:T(8,128)(2,1)} %bitcast_reduce_fusion) | data formatting | bytes 3145728 | tf_op jit(solution)/shard_map/reshape | solution.py:75
  309.4 0.4 convolution_multiply_fusion
  309.9 0.5 reshape.115
  310.4 1.9 copy.20
Async XLA Ops:
  7.2 126.2 %all-reduce.3.cloned.1.call-start = ((), (), s32[]{:S(2)}) async-start(), calls=%async_computation.2 | async-start | bytes 11010048
  7.2 0.7 copy-start.2
  7.2 1.9 copy-start.1
  7.2 126.1 %copy-start = (f32[28,12,1024]{2,0,1:T(8,128)S(1)}, f32[28,12,1024]{2,0,1:T(8,128)}, u32[]{:S(2)}) copy-start(f32[28,12,1024]{2,0,1:T(8,128)} %param.4) | copy-start | bytes 4128772
Sparse Core Ops, SparseCore 0:
  10.4 122.9 all-reduce.2
where the time goes:
time: 324 us; the launch traced here: 320 us
  waiting for transfers between devices  125 us (39%)
  blocking collectives  108 us (33%)
  local copies, waits for them, and re-layouts  40.1 us (12%)
  other arithmetic  18.2 us (6%)
  between operations  16 us (5%)
  matrix products  13 us (4%)
    unnamed x2, waiting for transfers between devices  125 us
    all_to_all x1, blocking collectives, local(): lax.all_to_all(outgoing, 'shard', split_axis=0, concat_axis=2, tiled=True)  62 us
    all_to_all x1, blocking collectives, send_back(): lax.all_to_all(orthogonal[None], 'shard', split_axis=2, concat_axis=0, ti...  45.7 us
    unnamed x13, local copies, waits for them, and re-layouts  16.7 us
    unnamed x1, other arithmetic  11.3 us
    all_to_all x1, local copies, waits for them, and re-layouts, send_back(): lax.all_to_all(orthogonal[None], 'shard', split_axis=2, concat_axis=0, ti...  10.4 us
    dot_general x2, matrix products, orthogonalize(): jnp.einsum('kfg,kgd->kfd', poly_term, iterate, preferred_element_type=jnp...  8.14 us
  transfers between devices with their start and end apart: 1, of which 1 were waited for; matrix products, arithmetic and copies ran while one was open for 0% of the time, Pallas kernels for 0%

commit v1 on v0

v1 whole, which is shorter than its diff:
```python
import functools
import math

import jax
import jax.numpy as jnp
from jax import lax
from jax.experimental import pallas as pl
from jax.experimental.pallas import tpu as pltpu
from jax.sharding import PartitionSpec as P


MESH = pl.DeviceIdType.MESH
BF = jnp.bfloat16
F32 = jnp.float32
I32 = jnp.int32

D, F = 1024, 768
NX, NY, NZ = 4, 4, 8
MROW = 28
CHUNKS, WIDE = 4, 256
HALF = WIDE // 2
SLOTS = 4
SCALE = 0.2 * math.sqrt(max(F, D))

momentum_decay = 0.95
epsilon_norm = 1e-07
coeff_first = 3.4445
coeff_second = -4.775
coeff_third = 2.0315


def iota(shape, axis):
    return lax.broadcasted_iota(I32, shape, axis)


def onehot(cond):
    return jnp.where(cond, 1.0, 0.0).astype(BF)


def dot(a, b):
    return jnp.dot(a, b, preferred_element_type=F32)


def dot_t(a, b):
    return lax.dot_general(a, b, (((1,), (1,)), ((), ())), preferred_element_type=F32)


def routes(owner, z_here):
    r0, r1 = iota((128, 128), 0), iota((128, 128), 1)
    owner = jnp.broadcast_to(owner[0:1], (128, 128))
    valid = r1 < MROW
    plane = jnp.where(valid, (owner >> 1) & 7, 99).astype(F32)
    place = jnp.where(valid, ((owner >> 4) << 1) | (owner & 1), 99).astype(F32)
    diag, before = r0 == r1, r0 < r1

    def column(row):
        return jnp.sum(jnp.where(diag, row, 0.0), axis=1, keepdims=True)

    def total(cond):
        return jnp.sum(jnp.where(cond, 1.0, 0.0), axis=0, keepdims=True)

    rank = total((column(plane) == plane) & before)
    valid = valid[0:1]
    home = valid & (rank < SLOTS)
    over = valid & (rank >= SLOTS)
    over_f = jnp.where(over, 1.0, 0.0)
    nth = total((column(jnp.broadcast_to(over_f, (128, 128))) > 0.5) & before)
    r0f = r0.astype(F32)
    count = jnp.sum(jnp.where(plane == r0f, 1.0, 0.0), axis=1, keepdims=True)
    taken = jnp.minimum(count, float(SLOTS))
    free = jnp.where(r0[:, 0:1] < NZ, float(SLOTS) - taken, 0.0)
    free_row = jnp.sum(jnp.where(diag, free, 0.0), axis=0, keepdims=True)
    first = jnp.sum(jnp.where(r1 < r0, free_row, 0.0), axis=1, keepdims=True)
    hit = (first <= nth) & (nth < first + free) & (r0 < NZ)
    away = jnp.sum(jnp.where(hit, r0f * SLOTS + taken + nth - first, 0.0), axis=0, keepdims=True)
    plane_row = plane[0:1]
    code = jnp.where(home, plane_row * SLOTS + rank, jnp.where(over, away, -1.0))
    code_over = jnp.where(over, plane_row * SLOTS + rank - SLOTS, -1.0)

    def tiled(row):
        row = jnp.where(valid, row, -1.0)
        wide = jnp.broadcast_to(row, (8, 128))
        out = wide
        for turn in (1, 2, 3):
            lane = iota((8, 128), 1)
            out = jnp.where((lane >> 5) == turn, pltpu.roll(wide, 32 * turn, 1), out)
        return out[0:1]

    same_row = ((r0 >> 2) & 3) == (r1 >> 5)
    wanted = ((r0 >> 4) * SLOTS + (r0 & 3)).astype(F32)
    forward = onehot(same_row & (tiled(code) == wanted))
    forward_over = onehot(same_row & (tiled(code_over) == wanted))
    code_col = jnp.sum(
        jnp.where(r1 == (r0 & 31), jnp.broadcast_to(code, (128, 128)), 0.0), axis=1, keepdims=True
    )
    code_col = jnp.where((r0[:, 0:1] & 31) < MROW, code_col, -1.0)
    back = onehot(
        ((r0 >> 5) == ((r1 >> 2) & 3)) & (code_col == ((r1 >> 4) * SLOTS + (r1 & 3)).astype(F32))
    )
    e0, e1 = iota((256, 128), 0), iota((256, 128), 1)
    mine = (place[0:1] == (e0 >> 5).astype(F32)) & (plane_row == z_here.astype(F32))
    pick = jnp.sum(jnp.where(mine, rank + 1.0, 0.0), axis=1, keepdims=True) - 1.0
    match = (((e0 >> 2) & 7) == (e1 >> 4)) & ((e0 & 3) == ((e1 >> 2) & 3))
    slot = (e1 & 3).astype(F32)
    give = onehot(match & (pick == slot))
    give_over = onehot(match & (pick == slot + SLOTS))
    return forward, forward_over, back, give, give_over


def kernel(
    grads_hbm,
    momentum_hbm,
    owners_ref,
    newm_ref,
    update_ref,
    owned_ref,
    grads,
    momentum,
    s_direct,
    s_far,
    s_comb,
    r_direct,
    r_far,
    r_comb,
    part,
    own,
    nest,
    zs_f,
    zr_f,
    zs_o,
    zr_o,
    zs_r,
    zr_r,
    ys_p,
    x_p,
    ys_r,
    yr_r,
    ys_o,
    x_o,
    x_a,
    x_b,
    gram_f,
    gram_b,
    poly_b,
    m_forward,
    m_over,
    m_back,
    m_give,
    m_give_over,
    load_sem,
    x_send,
    direct_sem,
    far_sem,
    comb_sem,
    z_send,
    zf_sem,
    zo_sem,
    zr_sem,
    y_send,
    yp_sem,
    yr_sem,
    yo_sem,
):
    x = lax.axis_index("dp")
    here = lax.axis_index("shard")
    y, z, c = here // 16, (here // 2) % NZ, here % 2
    e = 2 * y + c
    right, left, far = (x + 1) % NX, (x + 3) % NX, (x + 2) % NX

    def at(y_, z_, c_):
        return (x, (y_ * NZ + z_) * 2 + c_)

    def send(src, dst, send_sem, recv_sem, device):
        pltpu.make_async_remote_copy(
            src_ref=src, dst_ref=dst, send_sem=send_sem, recv_sem=recv_sem,
            device_id=device, device_id_type=MESH,
        ).start()

    def wait_recv(ref, sem):
        pltpu.make_async_remote_copy(
            src_ref=ref, dst_ref=ref, send_sem=sem, recv_sem=sem,
            device_id=(x, here), device_id_type=MESH,
        ).wait_recv()

    def wait_send(ref, sem):
        pltpu.make_async_remote_copy(
            src_ref=ref, dst_ref=ref, send_sem=sem, recv_sem=sem,
            device_id=(x, here), device_id_type=MESH,
        ).wait_send()

    def load(k):
        return pltpu.make_async_copy(
            grads_hbm.at[:, :, pl.ds(k * WIDE, WIDE)], grads.at[k], load_sem.at[k]
        )

    load_momentum = pltpu.make_async_copy(momentum_hbm, momentum, load_sem.at[CHUNKS])
    for k in range(CHUNKS):
        load(k).start()
    load_momentum.start()

    barrier = pltpu.get_barrier_semaphore()
    for device in ((right, here), (left, here)):
        pl.semaphore_signal(barrier, 1, device_id=device, device_id_type=MESH)
    for step in range(1, NZ):
        pl.semaphore_signal(barrier, 1, device_id=at(y, (z + step) % NZ, c), device_id_type=MESH)
    for step in range(1, 8):
        other = (e + step) % 8
        pl.semaphore_signal(
            barrier, 1, device_id=at(other // 2, z, other % 2), device_id_type=MESH
        )

    owner = pltpu.roll(jnp.broadcast_to(owners_ref[...], (8, 128)), (128 - MROW * x) % 128, 1)
    forward, forward_over, back, give, give_over = routes(owner, z)
    m_forward[...] = forward
    m_over[...] = forward_over
    m_back[...] = back
    m_give[...] = give
    m_give_over[...] = give_over
    nest[...] = jnp.zeros_like(nest)

    p0, p1 = iota((112, 128), 0), iota((112, 128), 1)
    quarter = (
        jnp.where(p0 >= 28, 1, 0) + jnp.where(p0 >= 56, 1, 0) + jnp.where(p0 >= 84, 1, 0)
    )

    def packing(parity):
        return onehot(p1 == p0 + 4 * quarter + 4 * parity)

    def window(k, to, table, g):
        start = pl.multiple_of(((MROW * to) // 8) * 8, 8)
        rows = grads[k, 4 * g : 4 * g + 4, pl.ds(start, 32), :].astype(BF).reshape(128, WIDE)
        return dot(table, rows)

    def pack(k):
        load(k).wait()
        odd = packing((x + 1) % 2)
        even = packing(x % 2)
        for g in range(3):
            v = window(k, far, even, g).astype(BF)
            s_far[0, k, g] = v[:, :HALF]
            s_far[1, k, g] = v[:, HALF:]
            v = window(k, right, odd, g)
            part[0, k, g] = v[:, :HALF]
            s_direct[0, k, g] = v[:, HALF:].astype(BF)
            v = window(k, left, odd, g)
            part[1, k, g] = v[:, HALF:]
            s_direct[1, k, g] = v[:, :HALF].astype(BF)

    def pack_own(k):
        even = packing(x % 2)
        for g in range(3):
            own[k, g] = window(k, x, even, g)

    towards = ((right, here), (left, here))

    def send_first(k):
        for way in range(2):
            send(s_far.at[way, k], r_far.at[way, k], x_send.at[0], far_sem.at[way, k], towards[way])
        for way in range(2):
            send(
                s_direct.at[way, k], r_direct.at[way, k], x_send.at[1], direct_sem.at[way, k],
                towards[way],
            )

    def send_combined(k):
        for way in range(2):
            wait_recv(r_far.at[way, k], far_sem.at[way, k])
            s_comb[way, k] = (part[way, k] + r_far[way, k].astype(F32)).astype(BF)
            send(
                s_comb.at[way, k], r_comb.at[way, k], x_send.at[2], comb_sem.at[way, k],
                towards[way],
            )

    def gradient(k):
        for way in range(2):
            wait_recv(r_direct.at[way, k], direct_sem.at[way, k])
            wait_recv(r_comb.at[way, k], comb_sem.at[way, k])
        low = own[k, :, :, :HALF] + r_direct[1, k].astype(F32) + r_comb[0, k].astype(F32)
        high = own[k, :, :, HALF:] + r_direct[0, k].astype(F32) + r_comb[1, k].astype(F32)
        own[k, :, :, :HALF] = low
        own[k, :, :, HALF:] = high
        for g in range(3):
            for rr in range(4):
                total = own[k, g, MROW * rr : MROW * (rr + 1), :]
                cols = slice(k * WIDE, (k + 1) * WIDE)
                moved = momentum_decay * momentum[4 * g + rr, :, cols] + total
                newm_ref[4 * g + rr, :, cols] = moved
                nest[g, 32 * rr : 32 * rr + MROW, :] = total + momentum_decay * moved

    def send_z(zs, zr, k, sem, recv_sem):
        zr[k, pl.ds(z, 1)] = zs[k, pl.ds(z, 1)]
        for step in (1, 7, 2, 6, 3, 5, 4):
            to = (z + step) % NZ
            send(zs.at[k, to], zr.at[k, z], sem, recv_sem.at[k], at(y, to, c))

    def forward_z(k):
        for g in range(3):
            rows = nest[g].astype(BF)
            zs_f[k, :, g] = dot(m_forward[...], rows).astype(BF).reshape(NZ, 16, WIDE)
        send_z(zs_f, zr_f, k, z_send.at[0], zf_sem)
        for g in range(3):
            rows = nest[g].astype(BF)
            zs_o[k, :, g] = dot(m_over[...], rows).astype(BF).reshape(NZ, 16, WIDE)
        send_z(zs_o, zr_o, k, z_send.at[1], zo_sem)

    i0, i1 = iota((128, 128), 0), iota((128, 128), 1)
    to_slots = lambda: onehot(i1 == ((i0 & 31) << 2) + (i0 >> 5))
    from_slots = lambda: onehot(i0 == ((i1 & 31) << 2) + (i1 >> 5))

    def others(n, me):
        return [(me + step) % n for step in range(1, n)]

    def relay_p(k):
        wait_recv(zr_f.at[k, pl.ds(0, 7)], zf_sem.at[k])
        table = to_slots()
        for g in range(3):
            rows = zr_f[k, :, g].reshape(128, WIDE)
            ys_p[k, :, g] = dot(table, rows).astype(BF).reshape(SLOTS, 32, WIDE)
        for to in others(NY, y):
            send(ys_p.at[k, to], x_p.at[k, e], y_send.at[0], yp_sem.at[k], at(to, z, 0))

        @pl.when(c == 0)
        def _():
            x_p[k, pl.ds(e, 1)] = ys_p[k, pl.ds(y, 1)]

        @pl.when(c == 1)
        def _():
            send(ys_p.at[k, y], x_p.at[k, e], y_send.at[1], yp_sem.at[k], at(y, z, 0))

    def matrix(ref, k):
        return ref[k].reshape(F, WIDE)

    def add_gram(src, k):
        rows = matrix(src, k)
        new = dot_t(rows, rows)
        gram_f[...] = new if k == 0 else gram_f[...] + new
        wide = rows.astype(F32)
        return jnp.sum(wide * wide)

    def poly():
        for i in range(3):
            block = gram_b[256 * i : 256 * (i + 1), :]
            square = dot(block, gram_b[...])
            poly_b[256 * i : 256 * (i + 1), :] = (
                coeff_second * block.astype(F32) + coeff_third * square
            ).astype(BF)

    def advance(src, dst, k):
        rows = matrix(src, k)
        out = coeff_first * rows.astype(F32) + dot(poly_b[...], rows)
        dst[k] = out.astype(BF).reshape(8, 3, 32, WIDE)

    def finish(src, dst, squares, done):
        inverse = 1.0 / (jnp.sqrt(squares) + epsilon_norm)
        gram_b[...] = (gram_f[...] * (inverse * inverse)).astype(BF)
        for k in range(CHUNKS):
            x_a[k] = (src[k].astype(F32) * inverse).astype(BF)
        poly()
        for k in range(CHUNKS):
            advance(x_a, x_b, k)
        for k in range(CHUNKS):
            add_gram_only(k)
        gram_b[...] = gram_f[...].astype(BF)
        poly()
        for k in range(CHUNKS):
            advance(x_b, dst, k)
            done(k)

    def add_gram_only(k):
        rows = matrix(x_b, k)
        new = dot_t(rows, rows)
        gram_f[...] = new if k == 0 else gram_f[...] + new

    def send_back(k):
        yr_r[k, pl.ds(y, 1)] = ys_r[k, pl.ds(e, 1)]
        for to in others(8, e):
            send(ys_r.at[k, to], yr_r.at[k, y], y_send.at[2], yr_sem.at[k], at(to // 2, z, to % 2))

    def primary():
        squares = 0.0
        for k in range(CHUNKS):
            wait_recv(x_p.at[k, pl.ds(0, 7)], yp_sem.at[k])
            squares = squares + add_gram(x_p, k)
        finish(x_p, ys_r, squares, send_back)

    def relay_o(k):
        wait_recv(zr_o.at[k, pl.ds(0, 7)], zo_sem.at[k])
        for g in range(3):
            rows = dot(m_give[...], zr_f[k, :, g].reshape(128, WIDE)) + dot(
                m_give_over[...], zr_o[k, :, g].reshape(128, WIDE)
            )
            ys_o[k, :, g] = rows.astype(BF).reshape(8, 32, WIDE)
        x_o[k, pl.ds(e, 1)] = ys_o[k, pl.ds(e, 1)]
        for to in others(8, e):
            send(ys_o.at[k, to], x_o.at[k, e], y_send.at[3], yo_sem.at[k], at(to // 2, z, to % 2))

    def relay_r(k):
        @pl.when(c == 0)
        def _():
            wait_recv(yr_r.at[k, pl.ds(0, 3)], yr_sem.at[k])

        @pl.when(c == 1)
        def _():
            wait_recv(yr_r.at[k, pl.ds(0, 4)], yr_sem.at[k])

        table = from_slots()
        for g in range(3):
            rows = yr_r[k, :, g].reshape(128, WIDE)
            zs_r[k, :, g] = dot(table, rows).astype(BF).reshape(NZ, 16, WIDE)
        send_z(zs_r, zr_r, k, z_send.at[2], zr_sem)

    def owner_part():
        squares = 0.0
        for k in range(CHUNKS):
            wait_recv(x_o.at[k, pl.ds(0, 7)], yo_sem.at[k])
            squares = squares + add_gram(x_o, k)

        t0, t1 = iota((192, 192), 0), iota((192, 192), 1)
        g0 = jnp.where((t1 % 96) >= 64, 2, jnp.where((t1 % 96) >= 32, 1, 0))
        c0 = jnp.where(t1 >= 96, 1, 0)
        place = ((t1 >> 2) & 7) * 24 + c0 * 12 + g0 * 4 + (t1 & 3)
        table = onehot(t0 == place)

        def done(k):
            for b in range(4):
                rows = x_a[k, 2 * b : 2 * b + 2].reshape(192, WIDE)
                owned_ref[192 * b : 192 * (b + 1), k * WIDE : (k + 1) * WIDE] = dot(
                    table, rows
                ).astype(BF)

        finish(x_o, x_a, squares, done)

    def unpack(k):
        wait_recv(zr_r.at[k, pl.ds(0, 7)], zr_sem.at[k])
        for g in range(3):
            rows = dot(m_back[...], zr_r[k, :, g].reshape(128, WIDE)) * SCALE
            rows = rows.reshape(4, 32, WIDE)
            update_ref[4 * g : 4 * g + 4, :, k * WIDE : (k + 1) * WIDE] = rows[:, :MROW, :]

    pack(0)
    pl.semaphore_wait(barrier, 16)
    send_first(0)
    pack(1)
    send_first(1)
    pack_own(0)
    load_momentum.wait()
    for k in range(CHUNKS):
        send_combined(k)
        if k + 2 < CHUNKS:
            pack(k + 2)
            send_first(k + 2)
        if k + 1 < CHUNKS:
            pack_own(k + 1)
        gradient(k)
        forward_z(k)
        if k >= 1:
            relay_p(k - 1)
    relay_p(CHUNKS - 1)

    @pl.when(c == 0)
    def _():
        primary()

    for k in range(CHUNKS):
        relay_o(k)
    for k in range(CHUNKS):
        relay_r(k)
    owner_part()
    for k in range(CHUNKS):
        unpack(k)

    wait_send(s_far, x_send.at[0])
    wait_send(s_direct, x_send.at[1])
    wait_send(s_comb, x_send.at[2])
    for i, ref in enumerate((zs_f, zs_o, zs_r)):
        wait_send(ref.at[:, pl.ds(0, 7)], z_send.at[i])
    wait_send(ys_p.at[:, pl.ds(0, 3)], y_send.at[0])

    @pl.when(c == 1)
    def _():
        wait_send(ys_p.at[:, 0], y_send.at[1])

    @pl.when(c == 0)
    def _():
        wait_send(ys_r.at[:, pl.ds(0, 7)], y_send.at[2])

    wait_send(ys_o.at[:, pl.ds(0, 7)], y_send.at[3])


def scratch():
    def vmem(*shape, dtype=BF):
        return pltpu.VMEM(shape, dtype)

    dma = pltpu.SemaphoreType.DMA
    x_half = (2, CHUNKS, 3, 112, HALF)
    z_all = (CHUNKS, NZ, 3, 16, WIDE)
    plane = (CHUNKS, 8, 3, 32, WIDE)
    quarter = (CHUNKS, SLOTS, 3, 32, WIDE)
    return [
        vmem(CHUNKS, 12, 112, WIDE, dtype=F32),
        vmem(12, MROW, D, dtype=F32),
        *[vmem(*x_half) for _ in range(6)],
        vmem(*x_half, dtype=F32),
        vmem(CHUNKS, 3, 112, WIDE, dtype=F32),
        vmem(3, 128, WIDE, dtype=F32),
        *[vmem(*z_all) for _ in range(6)],
        vmem(*quarter),
        vmem(*plane),
        vmem(*plane),
        vmem(*quarter),
        vmem(*plane),
        vmem(*plane),
        vmem(*plane),
        vmem(*plane),
        vmem(F, F, dtype=F32),
        vmem(F, F),
        vmem(F, F),
        vmem(128, 128),
        vmem(128, 128),
        vmem(128, 128),
        vmem(256, 128),
        vmem(256, 128),
        dma((CHUNKS + 1,)),
        dma((3,)),
        dma((2, CHUNKS)),
        dma((2, CHUNKS)),
        dma((2, CHUNKS)),
        dma((3,)),
        dma((CHUNKS,)),
        dma((CHUNKS,)),
        dma((CHUNKS,)),
        dma((4,)),
        dma((CHUNKS,)),
        dma((CHUNKS,)),
        dma((CHUNKS,)),
    ]


def local(partial_grads, momentum, owners):
    grads = jnp.transpose(partial_grads[0], (1, 0, 2))
    held = jnp.transpose(momentum, (1, 0, 2))
    owners = jnp.pad(owners, (0, 16)).reshape(1, 128)
    vmem = pl.BlockSpec(memory_space=pltpu.VMEM)
    anywhere = pl.BlockSpec(memory_space=pl.ANY)
    new_momentum, update, owned = pl.pallas_call(
        kernel,
        out_shape=(
            jax.ShapeDtypeStruct((12, MROW, D), F32),
            jax.ShapeDtypeStruct((12, MROW, D), F32),
            jax.ShapeDtypeStruct((F, D), BF),
        ),
        in_specs=[anywhere, anywhere, vmem],
        out_specs=(vmem, vmem, vmem),
        scratch_shapes=scratch(),
        compiler_params=pltpu.CompilerParams(
            collective_id=0, has_side_effects=True, vmem_limit_bytes=60 << 20
        ),
    )(grads, held, owners)
    return (
        jnp.transpose(new_momentum, (1, 0, 2)),
        jnp.transpose(update, (1, 0, 2)),
        owned[None, None],
    )


def solution(mesh):
    return jax.shard_map(
        local,
        mesh=mesh,
        in_specs=(P("dp", None, "shard", None), P("dp", "shard", None), P()),
        out_specs=(P("dp", "shard", None), P("dp", "shard", None), P("dp", "shard", None, None)),
        check_vma=False,
    )
```

time: 324 us -> 110 us (0.34); the launches traced: 320 us -> 110 us
  waiting for transfers between devices: 125 us -> 0 us
  blocking collectives: 108 us -> 0 us
  Pallas kernels: 0 us -> 102 us
  local copies, waits for them, and re-layouts: 40.1 us -> 7.14 us
  other arithmetic: 18.2 us -> 0 us
  between operations: 16 us -> 0.65 us
  matrix products: 13 us -> 0 us
    unnamed x2 -> x0, waiting for transfers between devices: 125 us -> none
    all_to_all x2 -> x0, blocking collectives: 108 us -> none  [the longest x1 62 us: local(): lax.all_to_all(outgoing, 'shard', split_axis=0, concat_axis=2, tiled=True)]
    pallas_call x0 -> x1, Pallas kernels: none -> 102 us  [local(): pl.pallas_call(kernel, out_shape=(jax.ShapeDtypeStruct((12, MROW, D), F32...]
    dot_general x6 -> x0, matrix products: 13 us -> none  [the longest x2 8.14 us: orthogonalize(): jnp.einsum('kfg,kgd->kfd', poly_term, iterate, preferred_element_type=jnp...]
    unnamed x1 -> x0, other arithmetic: 11.3 us -> none
    unnamed x13 -> x7, local copies, waits for them, and re-layouts: 16.7 us -> 5.97 us
    all_to_all x1 -> x0, local copies, waits for them, and re-layouts: 10.4 us -> none  [send_back(): lax.all_to_all(orthogonal[None], 'shard', split_axis=2, concat_axis=0, ti...]
    convert_element_type x2 -> x0, other arithmetic: 5.06 us -> none  [the longest x1 3.14 us: local(): nesterov = (gradient + momentum_decay * new_momentum).astype(jnp.bfloat16)]
  transfers between devices with their start and end apart: 1 -> 0, of which waited for: 1 -> 0; matrix products, arithmetic and copies ran while one was open for 0% -> 0% of each run, Pallas kernels for 0% -> 0%
where the time goes in v1:
time: 110 us
  Pallas kernels  102 us (93%)
  local copies, waits for them, and re-layouts  7.14 us (6%)
    pallas_call x1, Pallas kernels, local(): pl.pallas_call(kernel, out_shape=(jax.ShapeDtypeStruct((12, MROW, D), F32...  102 us
    unnamed x7, local copies, waits for them, and re-layouts  5.97 us

profile of v1, /device:TPU:1, one launch (start us, length us, event | category | flops | bytes accessed | tf_op | source)
XLA Modules:
  0.0 110.2 jit_solution(1666496772483765168)
XLA Ops:
  0.6 1.2 %pad_bitcast_fusion.owners_ref = s32[1,128]{1,0:T(1,128)} fusion(s32[112]{0:T(128)} %param.5), kind=kLoop, calls=%fused_computation | loop fusion | bytes 960 | tf_op jit(solution)/shard_map/reshape | solution.py:542
  1.8 102.4 %shard_map.58 = (f32[12,28,1024]{2,1,0:T(8,128)}, f32[12,28,1024]{2,1,0:T(8,128)}, bf16[768,1024]{1,0:T(8,128)(2,1)}) custom-call(f32[12,112,1024]{2,1,0:T(8,128)} %bitcast.9, f32[12,28,1024]{2,1,0:T(8,128)} %bitcast.10, s32[1,128]{1,0:T(1,128)} %pad_bitcast_fusion.owners_ref), custom_call_target="tpu_custom_call" | custom-call | tf_op jit(solution)/shard_map/pallas_call | solution.py:545
  104.2 0.0 copy-start.1
  104.2 2.8 %copy.9 = f32[28,12,1024]{2,0,1:T(8,128)} copy(f32[28,12,1024]{2,0,1:T(8,128)} %bitcast.13) | data formatting | bytes 2752512
  107.0 0.0 copy-done.1
  107.0 0.0 copy-start
  107.0 1.1 %copy.10 = f32[28,12,1024]{2,0,1:T(8,128)} copy(f32[28,12,1024]{2,0,1:T(8,128)S(1)} %bitcast.12) | data formatting | bytes 2752512
  108.2 0.8 copy-done
  109.0 1.1 %copy.11 = bf16[1,1,768,1024]{3,2,1,0:T(8,128)(2,1)} copy(bf16[1,1,768,1024]{3,2,1,0:T(8,128)(2,1)S(1)} %bitcast.11) | data formatting | bytes 3145728
Async XLA Ops:
  104.2 2.9 %copy-start.1 = (f32[12,28,1024]{2,1,0:T(8,128)S(1)}, f32[12,28,1024]{2,1,0:T(8,128)}, u32[]{:S(2)}) copy-start(f32[12,28,1024]{2,1,0:T(8,128)} %get-tuple-element.7) | copy-start | bytes 4128772
  107.0 2.0 %copy-start = (bf16[768,1024]{1,0:T(8,128)(2,1)S(1)}, bf16[768,1024]{1,0:T(8,128)(2,1)}, u32[]{:S(2)}) copy-start(bf16[768,1024]{1,0:T(8,128)(2,1)} %get-tuple-element.8) | copy-start | bytes 4718596

commit v2 on v1

--- a/solution.py
+++ b/solution.py
@@ -18,8 +18,9 @@
 NX, NY, NZ = 4, 4, 8
 MROW = 28
 CHUNKS, WIDE = 4, 256
-HALF = WIDE // 2
+HALF = NARROW = WIDE // 2
 SLOTS = 4
+PIECES = 4
 SCALE = 0.2 * math.sqrt(max(F, D))
 
 momentum_decay = 0.95
@@ -94,9 +95,9 @@
         jnp.where(r1 == (r0 & 31), jnp.broadcast_to(code, (128, 128)), 0.0), axis=1, keepdims=True
     )
     code_col = jnp.where((r0[:, 0:1] & 31) < MROW, code_col, -1.0)
-    back = onehot(
-        ((r0 >> 5) == ((r1 >> 2) & 3)) & (code_col == ((r1 >> 4) * SLOTS + (r1 & 3)).astype(F32))
-    )
+    b0, b1 = iota((128, 512), 0), iota((128, 512), 1)
+    whose = ((b0 >> 5) == ((b1 >> 2) & 3)) & (code_col == (b1 >> 4).astype(F32))
+    back = [onehot(whose & ((b1 & 3) == q)) for q in range(4)]
     e0, e1 = iota((256, 128), 0), iota((256, 128), 1)
     mine = (place[0:1] == (e0 >> 5).astype(F32)) & (plane_row == z_here.astype(F32))
     pick = jnp.sum(jnp.where(mine, rank + 1.0, 0.0), axis=1, keepdims=True) - 1.0
@@ -111,6 +112,9 @@
     grads_hbm,
     momentum_hbm,
     owners_ref,
+    newm_hbm,
+    update_hbm,
+    owned_hbm,
     newm_ref,
     update_ref,
     owned_ref,
@@ -133,8 +137,7 @@
     zr_r,
     ys_p,
     x_p,
-    ys_r,
-    yr_r,
+    x_d,
     ys_o,
     x_o,
     x_a,
@@ -148,6 +151,7 @@
     m_give,
     m_give_over,
     load_sem,
+    store_sem,
     x_send,
     direct_sem,
     far_sem,
@@ -155,11 +159,12 @@
     z_send,
     zf_sem,
     zo_sem,
+    r_send,
     zr_sem,
     y_send,
     yp_sem,
-    yr_sem,
     yo_sem,
+    all_in,
 ):
     x = lax.axis_index("dp")
     here = lax.axis_index("shard")
@@ -197,6 +202,13 @@
     for k in range(CHUNKS):
         load(k).start()
     load_momentum.start()
+
+    def store(i, k):
+        src, dst = ((newm_ref, newm_hbm), (update_ref, update_hbm))[i]
+        cols = pl.ds(k * WIDE, WIDE)
+        return pltpu.make_async_copy(src.at[:, :, cols], dst.at[:, :, cols], store_sem.at[i, k])
+
+    store_owned = pltpu.make_async_copy(owned_ref, owned_hbm, store_sem.at[2, 0])
 
     barrier = pltpu.get_barrier_semaphore()
     for device in ((right, here), (left, here)):
@@ -209,11 +221,13 @@
             barrier, 1, device_id=at(other // 2, z, other % 2), device_id_type=MESH
         )
 
-    owner = pltpu.roll(jnp.broadcast_to(owners_ref[...], (8, 128)), (128 - MROW * x) % 128, 1)
+    owner = jnp.concatenate([owners_ref[...], jnp.zeros((1, 16), I32)], axis=1)
+    owner = pltpu.roll(jnp.broadcast_to(owner, (8, 128)), (128 - MROW * x) % 128, 1)
     forward, forward_over, back, give, give_over = routes(owner, z)
     m_forward[...] = forward
     m_over[...] = forward_over
-    m_back[...] = back
+    for q in range(4):
+        m_back[128 * q : 128 * (q + 1)] = back[q]
     m_give[...] = give
     m_give_over[...] = give_over
     nest[...] = jnp.zeros_like(nest)
@@ -286,6 +300,7 @@
                 moved = momentum_decay * momentum[4 * g + rr, :, cols] + total
                 newm_ref[4 * g + rr, :, cols] = moved
                 nest[g, 32 * rr : 32 * rr + MROW, :] = total + momentum_decay * moved
+        store(0, k).start()
 
     def send_z(zs, zr, k, sem, recv_sem):
         zr[k, pl.ds(z, 1)] = zs[k, pl.ds(z, 1)]
@@ -301,6 +316,8 @@
         for g in range(3):
             rows = nest[g].astype(BF)
             zs_o[k, :, g] = dot(m_over[...], rows).astype(BF).reshape(NZ, 16, WIDE)
+
+    def forward_over_z(k):
         send_z(zs_o, zr_o, k, z_send.at[1], zo_sem)
 
     i0, i1 = iota((128, 128), 0), iota((128, 128), 1)
@@ -330,58 +347,119 @@
     def matrix(ref, k):
         return ref[k].reshape(F, WIDE)
 
+    blocks = [(i, j) for i in range(3) for j in range(i, 3)]
+
+    def block(ref, i, j):
+        return ref.at[256 * i : 256 * (i + 1), 256 * j : 256 * (j + 1)]
+
     def add_gram(src, k):
         rows = matrix(src, k)
-        new = dot_t(rows, rows)
-        gram_f[...] = new if k == 0 else gram_f[...] + new
-        wide = rows.astype(F32)
-        return jnp.sum(wide * wide)
+        for i, j in blocks:
+            new = dot_t(rows[256 * i : 256 * (i + 1)], rows[256 * j : 256 * (j + 1)])
+            into = block(gram_f, i, j)
+            into[...] = new if k == 0 else into[...] + new
+
+    def put_gram(i, j, value):
+        value = value.astype(BF)
+        block(gram_b, i, j)[...] = value
+        if i != j:
+            block(gram_b, j, i)[...] = value.T
+
+    def whole_gram(src):
+        for i, j in blocks:
+            total = 0.0
+            for k in range(CHUNKS):
+                rows = matrix(src, k)
+                total = total + dot_t(
+                    rows[256 * i : 256 * (i + 1)], rows[256 * j : 256 * (j + 1)]
+                )
+            put_gram(i, j, total)
 
     def poly():
-        for i in range(3):
-            block = gram_b[256 * i : 256 * (i + 1), :]
-            square = dot(block, gram_b[...])
-            poly_b[256 * i : 256 * (i + 1), :] = (
-                coeff_second * block.astype(F32) + coeff_third * square
-            ).astype(BF)
+        for i, j in blocks:
+            square = dot(
+                gram_b[256 * i : 256 * (i + 1), :], gram_b[:, 256 * j : 256 * (j + 1)]
+            )
+            value = coeff_second * block(gram_b, i, j)[...].astype(F32) + coeff_third * square
+            value = value.astype(BF)
+            block(poly_b, i, j)[...] = value
+            if i != j:
+                block(poly_b, j, i)[...] = value.T
 
     def advance(src, dst, k):
         rows = matrix(src, k)
         out = coeff_first * rows.astype(F32) + dot(poly_b[...], rows)
         dst[k] = out.astype(BF).reshape(8, 3, 32, WIDE)
 
-    def finish(src, dst, squares, done):
+    def finish(src, dst, done, between):
+        d0, d1 = iota((256, 256), 0), iota((256, 256), 1)
+        squares = 0.0
+        for i in range(3):
+            squares = squares + jnp.sum(jnp.where(d0 == d1, block(gram_f, i, i)[...], 0.0))
         inverse = 1.0 / (jnp.sqrt(squares) + epsilon_norm)
-        gram_b[...] = (gram_f[...] * (inverse * inverse)).astype(BF)
+        for i, j in blocks:
+            put_gram(i, j, block(gram_f, i, j)[...] * (inverse * inverse))
         for k in range(CHUNKS):
             x_a[k] = (src[k].astype(F32) * inverse).astype(BF)
         poly()
         for k in range(CHUNKS):
             advance(x_a, x_b, k)
-        for k in range(CHUNKS):
-            add_gram_only(k)
-        gram_b[...] = gram_f[...].astype(BF)
+        between()
+        whole_gram(x_b)
         poly()
         for k in range(CHUNKS):
             advance(x_b, dst, k)
             done(k)
 
-    def add_gram_only(k):
-        rows = matrix(x_b, k)
-        new = dot_t(rows, rows)
-        gram_f[...] = new if k == 0 else gram_f[...] + new
-
     def send_back(k):
-        yr_r[k, pl.ds(y, 1)] = ys_r[k, pl.ds(e, 1)]
-        for to in others(8, e):
-            send(ys_r.at[k, to], yr_r.at[k, y], y_send.at[2], yr_sem.at[k], at(to // 2, z, to % 2))
-
-    def primary():
-        squares = 0.0
-        for k in range(CHUNKS):
+        if k % 2 == 0:
+            return
+        half = k // 2
+        table = from_slots()
+
+        @pl.loop(0, 8)
+        def _(step):
+            to = (e + step) % 8
+            rows = jnp.concatenate(
+                [
+                    jnp.concatenate(
+                        [
+                            x_d[k - 1 + q // 2, to, g, :, NARROW * (q % 2) : NARROW * (q % 2 + 1)]
+                            for g in range(3)
+                        ],
+                        axis=1,
+                    )
+                    for q in range(4)
+                ],
+                axis=0,
+            )
+            rows = dot(table, rows).astype(BF).reshape(NZ, 16, 3 * NARROW)
+            zs_r[half, pl.ds(to * NZ, NZ)] = rows
+
+            for near in (0, 1, 7, 2, 6, 3, 5, 4):
+                to_z = (z + near) % NZ
+
+                def give():
+                    send(
+                        zs_r.at[half, to * NZ + to_z], zr_r.at[half, z * SLOTS + y], r_send,
+                        zr_sem.at[half], at(to // 2, to_z, to % 2),
+                    )
+
+                if near == 0:
+
+                    @pl.when(step > 0)
+                    def _():
+                        give()
+                else:
+                    give()
+
+        zr_r[half, pl.ds(z * SLOTS + y, 1)] = zs_r[half, pl.ds(e * NZ + z, 1)]
+
+    def primary_gram(k):
+        @pl.when(c == 0)
+        def _():
             wait_recv(x_p.at[k, pl.ds(0, 7)], yp_sem.at[k])
-            squares = squares + add_gram(x_p, k)
-        finish(x_p, ys_r, squares, send_back)
+            add_gram(x_p, k)
 
     def relay_o(k):
         wait_recv(zr_o.at[k, pl.ds(0, 7)], zo_sem.at[k])
@@ -392,28 +470,12 @@
             ys_o[k, :, g] = rows.astype(BF).reshape(8, 32, WIDE)
         x_o[k, pl.ds(e, 1)] = ys_o[k, pl.ds(e, 1)]
         for to in others(8, e):
-            send(ys_o.at[k, to], x_o.at[k, e], y_send.at[3], yo_sem.at[k], at(to // 2, z, to % 2))
-
-    def relay_r(k):
-        @pl.when(c == 0)
-        def _():
-            wait_recv(yr_r.at[k, pl.ds(0, 3)], yr_sem.at[k])
-
-        @pl.when(c == 1)
-        def _():
-            wait_recv(yr_r.at[k, pl.ds(0, 4)], yr_sem.at[k])
-
-        table = from_slots()
-        for g in range(3):
-            rows = yr_r[k, :, g].reshape(128, WIDE)
-            zs_r[k, :, g] = dot(table, rows).astype(BF).reshape(NZ, 16, WIDE)
-        send_z(zs_r, zr_r, k, z_send.at[2], zr_sem)
+            send(ys_o.at[k, to], x_o.at[k, e], y_send.at[2], yo_sem.at[k], at(to // 2, z, to % 2))
 
     def owner_part():
-        squares = 0.0
         for k in range(CHUNKS):
             wait_recv(x_o.at[k, pl.ds(0, 7)], yo_sem.at[k])
-            squares = squares + add_gram(x_o, k)
+            add_gram(x_o, k)
 
         t0, t1 = iota((192, 192), 0), iota((192, 192), 1)
         g0 = jnp.where((t1 % 96) >= 64, 2, jnp.where((t1 % 96) >= 32, 1, 0))
@@ -428,51 +490,92 @@
                     table, rows
                 ).astype(BF)
 
-        finish(x_o, x_a, squares, done)
-
-    def unpack(k):
-        wait_recv(zr_r.at[k, pl.ds(0, 7)], zr_sem.at[k])
-        for g in range(3):
-            rows = dot(m_back[...], zr_r[k, :, g].reshape(128, WIDE)) * SCALE
-            rows = rows.reshape(4, 32, WIDE)
-            update_ref[4 * g : 4 * g + 4, :, k * WIDE : (k + 1) * WIDE] = rows[:, :MROW, :]
+        finish(x_o, x_a, done, lambda: None)
+        store_owned.start()
+
+    def unpack(half):
+        @pl.when(c == 0)
+        def _():
+            wait_recv(zr_r.at[half, pl.ds(0, 31)], zr_sem.at[half])
+
+        @pl.when(c == 1)
+        def _():
+            wait_recv(zr_r.at[half, pl.ds(0, 32)], zr_sem.at[half])
+
+        for q in range(4):
+            rows = zr_r[half].reshape(512, 3 * NARROW)
+            rows = dot(m_back[128 * q : 128 * (q + 1)], rows) * SCALE
+            for g in range(3):
+                for rr in range(4):
+                    first = 512 * half + NARROW * q
+                    update_ref[4 * g + rr, :, first : first + NARROW] = rows[
+                        32 * rr : 32 * rr + MROW, NARROW * g : NARROW * (g + 1)
+                    ]
+        for k in (2 * half, 2 * half + 1):
+            store(1, k).start()
 
     pack(0)
     pl.semaphore_wait(barrier, 16)
+    for step in range(1, NZ):
+        pl.semaphore_signal(all_in, 1, device_id=at(y, (z + step) % NZ, c), device_id_type=MESH)
     send_first(0)
     pack(1)
     send_first(1)
+    send_combined(0)
+    pack(2)
+    send_first(2)
     pack_own(0)
     load_momentum.wait()
     for k in range(CHUNKS):
-        send_combined(k)
-        if k + 2 < CHUNKS:
-            pack(k + 2)
-            send_first(k + 2)
+        if k + 1 < CHUNKS:
+            send_combined(k + 1)
+        if k + 3 < CHUNKS:
+            pack(k + 3)
+            send_first(k + 3)
         if k + 1 < CHUNKS:
             pack_own(k + 1)
         gradient(k)
         forward_z(k)
         if k >= 1:
             relay_p(k - 1)
+        if k >= 2:
+            primary_gram(k - 2)
+    forward_over_z(0)
+    forward_over_z(1)
     relay_p(CHUNKS - 1)
+    forward_over_z(2)
+    forward_over_z(3)
+    primary_gram(CHUNKS - 2)
+    primary_gram(CHUNKS - 1)
+    pl.semaphore_wait(all_in, NZ - 1)
 
     @pl.when(c == 0)
     def _():
-        primary()
-
+        def between():
+            relay_o(0)
+            relay_o(1)
+
+        finish(x_p, x_d, send_back, between)
+
+    @pl.when(c == 1)
+    def _():
+        relay_o(0)
+        relay_o(1)
+
+    relay_o(2)
+    relay_o(3)
+    owner_part()
+    for half in range(2):
+        unpack(half)
     for k in range(CHUNKS):
-        relay_o(k)
-    for k in range(CHUNKS):
-        relay_r(k)
-    owner_part()
-    for k in range(CHUNKS):
-        unpack(k)
+        store(0, k).wait()
+        store(1, k).wait()
+    store_owned.wait()
 
     wait_send(s_far, x_send.at[0])
     wait_send(s_direct, x_send.at[1])
     wait_send(s_comb, x_send.at[2])
-    for i, ref in enumerate((zs_f, zs_o, zs_r)):
+    for i, ref in enumerate((zs_f, zs_o)):
         wait_send(ref.at[:, pl.ds(0, 7)], z_send.at[i])
     wait_send(ys_p.at[:, pl.ds(0, 3)], y_send.at[0])
 
@@ -482,9 +585,9 @@
 
     @pl.when(c == 0)
     def _():
-        wait_send(ys_r.at[:, pl.ds(0, 7)], y_send.at[2])
-
-    wait_send(ys_o.at[:, pl.ds(0, 7)], y_send.at[3])
+        wait_send(zs_r.at[:, pl.ds(0, 63)], r_send)
+
+    wait_send(ys_o.at[:, pl.ds(0, 7)], y_send.at[2])
 
 
 def scratch():
@@ -497,17 +600,21 @@
     plane = (CHUNKS, 8, 3, 32, WIDE)
     quarter = (CHUNKS, SLOTS, 3, 32, WIDE)
     return [
+        vmem(12, MROW, D, dtype=F32),
+        vmem(12, MROW, D, dtype=F32),
+        vmem(F, D),
         vmem(CHUNKS, 12, 112, WIDE, dtype=F32),
         vmem(12, MROW, D, dtype=F32),
         *[vmem(*x_half) for _ in range(6)],
         vmem(*x_half, dtype=F32),
         vmem(CHUNKS, 3, 112, WIDE, dtype=F32),
         vmem(3, 128, WIDE, dtype=F32),
-        *[vmem(*z_all) for _ in range(6)],
+        *[vmem(*z_all) for _ in range(4)],
+        vmem(2, 64, 16, 3 * NARROW),
+        vmem(2, 32, 16, 3 * NARROW),
         vmem(*quarter),
         vmem(*plane),
         vmem(*plane),
-        vmem(*quarter),
         vmem(*plane),
         vmem(*plane),
         vmem(*plane),
@@ -517,45 +624,76 @@
         vmem(F, F),
         vmem(128, 128),
         vmem(128, 128),
-        vmem(128, 128),
+        vmem(512, 512),
         vmem(256, 128),
         vmem(256, 128),
         dma((CHUNKS + 1,)),
+        dma((3, CHUNKS)),
         dma((3,)),
         dma((2, CHUNKS)),
         dma((2, CHUNKS)),
         dma((2, CHUNKS)),
+        dma((2,)),
+        dma((CHUNKS,)),
+        dma((CHUNKS,)),
+        dma(()),
+        dma((2,)),
         dma((3,)),
         dma((CHUNKS,)),
         dma((CHUNKS,)),
-        dma((CHUNKS,)),
-        dma((4,)),
-        dma((CHUNKS,)),
-        dma((CHUNKS,)),
-        dma((CHUNKS,)),
+        pltpu.SemaphoreType.REGULAR,
     ]
+
+
+def hand_over(*refs):
+    srcs, dsts, held = refs[:3], refs[3:6], refs[6:9]
+    in_sem, out_sem = refs[9:]
+
+    def move(i, piece, src, dst, sem):
+        rows = src.shape[0] // PIECES
+        part = pl.ds(piece * rows, rows)
+        return pltpu.make_async_copy(src.at[part], dst.at[part], sem.at[i, piece])
+
+    each = [(i, piece) for i in range(3) for piece in range(PIECES)]
+    for i, piece in each:
+        move(i, piece, srcs[i], held[i], in_sem).start()
+    for i, piece in each:
+        move(i, piece, srcs[i], held[i], in_sem).wait()
+        move(i, piece, held[i], dsts[i], out_sem).start()
+    for i, piece in each:
+        move(i, piece, held[i], dsts[i], out_sem).wait()
 
 
 def local(partial_grads, momentum, owners):
     grads = jnp.transpose(partial_grads[0], (1, 0, 2))
     held = jnp.transpose(momentum, (1, 0, 2))
-    owners = jnp.pad(owners, (0, 16)).reshape(1, 128)
+    owners = owners.reshape(1, 112)
     vmem = pl.BlockSpec(memory_space=pltpu.VMEM)
     anywhere = pl.BlockSpec(memory_space=pl.ANY)
-    new_momentum, update, owned = pl.pallas_call(
+    outs = (
+        jax.ShapeDtypeStruct((12, MROW, D), F32),
+        jax.ShapeDtypeStruct((12, MROW, D), F32),
+        jax.ShapeDtypeStruct((F, D), BF),
+    )
+    results = pl.pallas_call(
         kernel,
-        out_shape=(
-            jax.ShapeDtypeStruct((12, MROW, D), F32),
-            jax.ShapeDtypeStruct((12, MROW, D), F32),
-            jax.ShapeDtypeStruct((F, D), BF),
-        ),
+        out_shape=outs,
         in_specs=[anywhere, anywhere, vmem],
-        out_specs=(vmem, vmem, vmem),
+        out_specs=(anywhere,) * 3,
         scratch_shapes=scratch(),
         compiler_params=pltpu.CompilerParams(
             collective_id=0, has_side_effects=True, vmem_limit_bytes=60 << 20
         ),
     )(grads, held, owners)
+    new_momentum, update, owned = pl.pallas_call(
+        hand_over,
+        out_shape=outs,
+        in_specs=[anywhere] * 3,
+        out_specs=(anywhere,) * 3,
+        scratch_shapes=[pltpu.VMEM(out.shape, out.dtype) for out in outs]
+        + [pltpu.SemaphoreType.DMA((3, PIECES))] * 2,
+        compiler_params=pltpu.CompilerParams(vmem_limit_bytes=60 << 20),
+    )(*results)
     return (
         jnp.transpose(new_momentum, (1, 0, 2)),
         jnp.transpose(update, (1, 0, 2)),

time: 110 us -> 91.7 us (0.83); the launches traced: 110 us -> 90.6 us
  Pallas kernels: 102 us -> 89.8 us
  local copies, waits for them, and re-layouts: 7.14 us -> 0 us
    pallas_call x1 -> x2, Pallas kernels: 102 us -> 89.8 us  [the longest x1 85.6 us: local(): pl.pallas_call(kernel, out_shape=outs, in_specs=[anywhere, anywhere, vmem...]
    unnamed x7 -> x0, local copies, waits for them, and re-layouts: 5.97 us -> none
    reshape x1 -> x0, local copies, waits for them, and re-layouts: 1.17 us -> none  [local(): owners = jnp.pad(owners, (0, 16)).reshape(1, 128)]
where the time goes in v2:
time: 91.7 us; the launch traced here: 90.6 us
  Pallas kernels  89.8 us (98%)
    pallas_call x1, Pallas kernels, local(): pl.pallas_call(kernel, out_shape=outs, in_specs=[anywhere, anywhere, vmem...  85.6 us
    pallas_call x1, Pallas kernels, local(): pl.pallas_call(hand_over, out_shape=outs, in_specs=[anywhere] * 3, out_sp...  4.27 us

profile of v2, /device:TPU:1, one launch (start us, length us, event | category | flops | bytes accessed | tf_op | source)
XLA Modules:
  0.0 90.6 jit_solution(10536398953226037446)
XLA Ops:
  0.6 85.6 %shard_map.58 = (f32[12,28,1024]{2,1,0:T(8,128)}, f32[12,28,1024]{2,1,0:T(8,128)}, bf16[768,1024]{1,0:T(8,128)(2,1)}) custom-call(f32[12,112,1024]{2,1,0:T(8,128)} %bitcast.8, f32[12,28,1024]{2,1,0:T(8,128)} %bitcast.9, s32[1,112]{1,0:T(1,128)} %bitcast.10), custom_call_target="tpu_custom_call" | custom-call | tf_op jit(solution)/shard_map/pallas_call | solution.py:678
  86.2 4.3 %shard_map.59 = (f32[12,28,1024]{2,1,0:T(8,128)}, f32[12,28,1024]{2,1,0:T(8,128)}, bf16[768,1024]{1,0:T(8,128)(2,1)}) custom-call(f32[12,28,1024]{2,1,0:T(8,128)} %get-tuple-element.9.refs_0_, f32[12,28,1024]{2,1,0:T(8,128)} %get-tuple-element.10.refs_1_, bf16[768,1024]{1,0:T(8,128)(2,1)} %get-tuple-element.11.refs_2_), custom_call_target="tpu_custom_call" | custom-call | tf_op jit(solution)/shard_map/pallas_call | solution.py:688

commit v3 on v2

--- a/solution.py
+++ b/solution.py
@@ -46,37 +46,35 @@
     return lax.dot_general(a, b, (((1,), (1,)), ((), ())), preferred_element_type=F32)
 
 
-def routes(owner, z_here):
+def routes(owner, chip_here):
     r0, r1 = iota((128, 128), 0), iota((128, 128), 1)
     owner = jnp.broadcast_to(owner[0:1], (128, 128))
     valid = r1 < MROW
-    plane = jnp.where(valid, (owner >> 1) & 7, 99).astype(F32)
-    place = jnp.where(valid, ((owner >> 4) << 1) | (owner & 1), 99).astype(F32)
+    chip = jnp.where(valid, ((owner >> 1) & 7) * SLOTS + (owner >> 4), -1).astype(F32)
+    core = jnp.where(valid, owner & 1, -1)
+    first, second = core == 0, core == 1
     diag, before = r0 == r1, r0 < r1
-
-    def column(row):
-        return jnp.sum(jnp.where(diag, row, 0.0), axis=1, keepdims=True)
-
-    def total(cond):
-        return jnp.sum(jnp.where(cond, 1.0, 0.0), axis=0, keepdims=True)
-
-    rank = total((column(plane) == plane) & before)
-    valid = valid[0:1]
-    home = valid & (rank < SLOTS)
-    over = valid & (rank >= SLOTS)
-    over_f = jnp.where(over, 1.0, 0.0)
-    nth = total((column(jnp.broadcast_to(over_f, (128, 128))) > 0.5) & before)
     r0f = r0.astype(F32)
-    count = jnp.sum(jnp.where(plane == r0f, 1.0, 0.0), axis=1, keepdims=True)
-    taken = jnp.minimum(count, float(SLOTS))
-    free = jnp.where(r0[:, 0:1] < NZ, float(SLOTS) - taken, 0.0)
-    free_row = jnp.sum(jnp.where(diag, free, 0.0), axis=0, keepdims=True)
-    first = jnp.sum(jnp.where(r1 < r0, free_row, 0.0), axis=1, keepdims=True)
-    hit = (first <= nth) & (nth < first + free) & (r0 < NZ)
-    away = jnp.sum(jnp.where(hit, r0f * SLOTS + taken + nth - first, 0.0), axis=0, keepdims=True)
-    plane_row = plane[0:1]
-    code = jnp.where(home, plane_row * SLOTS + rank, jnp.where(over, away, -1.0))
-    code_over = jnp.where(over, plane_row * SLOTS + rank - SLOTS, -1.0)
+
+    def over_rows(cond, value=1.0):
+        return jnp.sum(jnp.where(cond, value, 0.0), axis=0, keepdims=True)
+
+    def over_lanes(cond, value=1.0):
+        return jnp.sum(jnp.where(cond, value, 0.0), axis=1, keepdims=True)
+
+    second_col = over_lanes(diag & second)
+    nth = over_rows(before & (second_col > 0.5))
+    taken = over_lanes(first & (chip == r0f))
+    free = jnp.where((r0[:, 0:1] < NZ * SLOTS) & (taken < 0.5), 1.0, 0.0)
+    free_row = over_rows(diag & (free > 0.5))
+    free_before = over_lanes((r1 < r0) & (free_row > 0.5))
+    away = over_rows((free > 0.5) & (free_before == nth), r0f)
+    first, second, valid, chip = first[0:1], second[0:1], valid[0:1], chip[0:1]
+    code = jnp.where(first, chip, jnp.where(second, away, -1.0))
+    code_over = jnp.where(second, chip, -1.0)
+    owns = jnp.sum(
+        jnp.where(first & (chip == chip_here.astype(F32)), 1.0, 0.0), axis=1, keepdims=True
+    )
 
     def tiled(row):
         row = jnp.where(valid, row, -1.0)
@@ -98,14 +96,7 @@
     b0, b1 = iota((128, 512), 0), iota((128, 512), 1)
     whose = ((b0 >> 5) == ((b1 >> 2) & 3)) & (code_col == (b1 >> 4).astype(F32))
     back = [onehot(whose & ((b1 & 3) == q)) for q in range(4)]
-    e0, e1 = iota((256, 128), 0), iota((256, 128), 1)
-    mine = (place[0:1] == (e0 >> 5).astype(F32)) & (plane_row == z_here.astype(F32))
-    pick = jnp.sum(jnp.where(mine, rank + 1.0, 0.0), axis=1, keepdims=True) - 1.0
-    match = (((e0 >> 2) & 7) == (e1 >> 4)) & ((e0 & 3) == ((e1 >> 2) & 3))
-    slot = (e1 & 3).astype(F32)
-    give = onehot(match & (pick == slot))
-    give_over = onehot(match & (pick == slot + SLOTS))
-    return forward, forward_over, back, give, give_over
+    return forward, forward_over, back, owns
 
 
 def kernel(
@@ -136,10 +127,9 @@
     zs_r,
     zr_r,
     ys_p,
-    x_p,
+    x_in,
     x_d,
     ys_o,
-    x_o,
     x_a,
     x_b,
     gram_f,
@@ -148,8 +138,7 @@
     m_forward,
     m_over,
     m_back,
-    m_give,
-    m_give_over,
+    m_owns,
     load_sem,
     store_sem,
     x_send,
@@ -162,8 +151,7 @@
     r_send,
     zr_sem,
     y_send,
-    yp_sem,
-    yo_sem,
+    in_sem,
     all_in,
 ):
     x = lax.axis_index("dp")
@@ -223,13 +211,12 @@
 
     owner = jnp.concatenate([owners_ref[...], jnp.zeros((1, 16), I32)], axis=1)
     owner = pltpu.roll(jnp.broadcast_to(owner, (8, 128)), (128 - MROW * x) % 128, 1)
-    forward, forward_over, back, give, give_over = routes(owner, z)
+    forward, forward_over, back, owns = routes(owner, z * SLOTS + y)
     m_forward[...] = forward
     m_over[...] = forward_over
     for q in range(4):
         m_back[128 * q : 128 * (q + 1)] = back[q]
-    m_give[...] = give
-    m_give_over[...] = give_over
+    m_owns[...] = jnp.broadcast_to(owns, (8, 128))
     nest[...] = jnp.zeros_like(nest)
 
     p0, p1 = iota((112, 128), 0), iota((112, 128), 1)
@@ -327,22 +314,29 @@
     def others(n, me):
         return [(me + step) % n for step in range(1, n)]
 
+    def relay(k, zr, ys, sem, core):
+        table = to_slots()
+        for g in range(3):
+            rows = zr[k, :, g].reshape(128, WIDE)
+            ys[k, :, g] = dot(table, rows).astype(BF).reshape(SLOTS, 32, WIDE)
+        for to in others(NY, y):
+            send(ys.at[k, to], x_in.at[k, e], y_send.at[sem], in_sem.at[k], at(to, z, core))
+
+        @pl.when(c == core)
+        def _():
+            x_in[k, pl.ds(e, 1)] = ys[k, pl.ds(y, 1)]
+
+        @pl.when(c != core)
+        def _():
+            send(ys.at[k, y], x_in.at[k, e], y_send.at[sem + 1], in_sem.at[k], at(y, z, core))
+
     def relay_p(k):
         wait_recv(zr_f.at[k, pl.ds(0, 7)], zf_sem.at[k])
-        table = to_slots()
-        for g in range(3):
-            rows = zr_f[k, :, g].reshape(128, WIDE)
-            ys_p[k, :, g] = dot(table, rows).astype(BF).reshape(SLOTS, 32, WIDE)
-        for to in others(NY, y):
-            send(ys_p.at[k, to], x_p.at[k, e], y_send.at[0], yp_sem.at[k], at(to, z, 0))
-
-        @pl.when(c == 0)
-        def _():
-            x_p[k, pl.ds(e, 1)] = ys_p[k, pl.ds(y, 1)]
-
-        @pl.when(c == 1)
-        def _():
-            send(ys_p.at[k, y], x_p.at[k, e], y_send.at[1], yp_sem.at[k], at(y, z, 0))
+        relay(k, zr_f, ys_p, 0, 0)
+
+    def relay_o(k):
+        wait_recv(zr_o.at[k, pl.ds(0, 7)], zo_sem.at[k])
+        relay(k, zr_o, ys_o, 2, 1)
 
     def matrix(ref, k):
         return ref[k].reshape(F, WIDE)
@@ -455,42 +449,28 @@
 
         zr_r[half, pl.ds(z * SLOTS + y, 1)] = zs_r[half, pl.ds(e * NZ + z, 1)]
 
+    def gram_in(k):
+        wait_recv(x_in.at[k, pl.ds(0, 7)], in_sem.at[k])
+        add_gram(x_in, k)
+
     def primary_gram(k):
         @pl.when(c == 0)
         def _():
-            wait_recv(x_p.at[k, pl.ds(0, 7)], yp_sem.at[k])
-            add_gram(x_p, k)
-
-    def relay_o(k):
-        wait_recv(zr_o.at[k, pl.ds(0, 7)], zo_sem.at[k])
-        for g in range(3):
-            rows = dot(m_give[...], zr_f[k, :, g].reshape(128, WIDE)) + dot(
-                m_give_over[...], zr_o[k, :, g].reshape(128, WIDE)
-            )
-            ys_o[k, :, g] = rows.astype(BF).reshape(8, 32, WIDE)
-        x_o[k, pl.ds(e, 1)] = ys_o[k, pl.ds(e, 1)]
-        for to in others(8, e):
-            send(ys_o.at[k, to], x_o.at[k, e], y_send.at[2], yo_sem.at[k], at(to // 2, z, to % 2))
-
-    def owner_part():
-        for k in range(CHUNKS):
-            wait_recv(x_o.at[k, pl.ds(0, 7)], yo_sem.at[k])
-            add_gram(x_o, k)
-
+            gram_in(k)
+
+    def put_owned():
         t0, t1 = iota((192, 192), 0), iota((192, 192), 1)
         g0 = jnp.where((t1 % 96) >= 64, 2, jnp.where((t1 % 96) >= 32, 1, 0))
         c0 = jnp.where(t1 >= 96, 1, 0)
         place = ((t1 >> 2) & 7) * 24 + c0 * 12 + g0 * 4 + (t1 & 3)
-        table = onehot(t0 == place)
-
-        def done(k):
+        kept = (m_owns[0:1, 0:1] > 0.5) | (c == 1)
+        table = onehot((t0 == place) & kept)
+        for k in range(CHUNKS):
             for b in range(4):
-                rows = x_a[k, 2 * b : 2 * b + 2].reshape(192, WIDE)
+                rows = x_d[k, 2 * b : 2 * b + 2].reshape(192, WIDE)
                 owned_ref[192 * b : 192 * (b + 1), k * WIDE : (k + 1) * WIDE] = dot(
                     table, rows
                 ).astype(BF)
-
-        finish(x_o, x_a, done, lambda: None)
         store_owned.start()
 
     def unpack(half):
@@ -555,16 +535,19 @@
             relay_o(0)
             relay_o(1)
 
-        finish(x_p, x_d, send_back, between)
+        finish(x_in, x_d, send_back, between)
+        relay_o(2)
+        relay_o(3)
 
     @pl.when(c == 1)
     def _():
-        relay_o(0)
-        relay_o(1)
-
-    relay_o(2)
-    relay_o(3)
-    owner_part()
+        for k in range(CHUNKS):
+            relay_o(k)
+        for k in range(CHUNKS):
+            gram_in(k)
+        finish(x_in, x_d, lambda k: None, lambda: None)
+
+    put_owned()
     for half in range(2):
         unpack(half)
     for k in range(CHUNKS):
@@ -578,6 +561,7 @@
     for i, ref in enumerate((zs_f, zs_o)):
         wait_send(ref.at[:, pl.ds(0, 7)], z_send.at[i])
     wait_send(ys_p.at[:, pl.ds(0, 3)], y_send.at[0])
+    wait_send(ys_o.at[:, pl.ds(0, 3)], y_send.at[2])
 
     @pl.when(c == 1)
     def _():
@@ -585,9 +569,8 @@
 
     @pl.when(c == 0)
     def _():
+        wait_send(ys_o.at[:, 0], y_send.at[3])
         wait_send(zs_r.at[:, pl.ds(0, 63)], r_send)
-
-    wait_send(ys_o.at[:, pl.ds(0, 7)], y_send.at[2])
 
 
 def scratch():
@@ -615,8 +598,7 @@
         vmem(*quarter),
         vmem(*plane),
         vmem(*plane),
-        vmem(*plane),
-        vmem(*plane),
+        vmem(*quarter),
         vmem(*plane),
         vmem(*plane),
         vmem(F, F, dtype=F32),
@@ -625,8 +607,7 @@
         vmem(128, 128),
         vmem(128, 128),
         vmem(512, 512),
-        vmem(256, 128),
-        vmem(256, 128),
+        vmem(8, 128, dtype=F32),
         dma((CHUNKS + 1,)),
         dma((3, CHUNKS)),
         dma((3,)),
@@ -638,8 +619,7 @@
         dma((CHUNKS,)),
         dma(()),
         dma((2,)),
-        dma((3,)),
-        dma((CHUNKS,)),
+        dma((4,)),
         dma((CHUNKS,)),
         pltpu.SemaphoreType.REGULAR,
     ]

time: 91.7 us -> 86.8 us (0.947); the launches traced: 90.6 us -> 86.7 us
  Pallas kernels: 89.8 us -> 85.9 us
    pallas_call x1, Pallas kernels: 85.6 us -> 81.6 us  [local(): pl.pallas_call(kernel, out_shape=outs, in_specs=[anywhere, anywhere, vmem...]
where the time goes in v3:
time: 86.8 us; the launch traced here: 86.7 us
  Pallas kernels  85.9 us (99%)
    pallas_call x1, Pallas kernels, local(): pl.pallas_call(kernel, out_shape=outs, in_specs=[anywhere, anywhere, vmem...  81.6 us
    pallas_call x1, Pallas kernels, local(): pl.pallas_call(hand_over, out_shape=outs, in_specs=[anywhere] * 3, out_sp...  4.27 us

profile of v3, /device:TPU:1, one launch (start us, length us, event | category | flops | bytes accessed | tf_op | source)
XLA Modules:
  0.0 86.7 jit_solution(10290563475743617586)
XLA Ops:
  0.6 81.6 %shard_map.58 = (f32[12,28,1024]{2,1,0:T(8,128)}, f32[12,28,1024]{2,1,0:T(8,128)}, bf16[768,1024]{1,0:T(8,128)(2,1)}) custom-call(f32[12,112,1024]{2,1,0:T(8,128)} %bitcast.8, f32[12,28,1024]{2,1,0:T(8,128)} %bitcast.9, s32[1,112]{1,0:T(1,128)} %bitcast.10), custom_call_target="tpu_custom_call" | custom-call | tf_op jit(solution)/shard_map/pallas_call | solution.py:658
  82.3 4.3 %shard_map.59 = (f32[12,28,1024]{2,1,0:T(8,128)}, f32[12,28,1024]{2,1,0:T(8,128)}, bf16[768,1024]{1,0:T(8,128)(2,1)}) custom-call(f32[12,28,1024]{2,1,0:T(8,128)} %get-tuple-element.9.refs_0_, f32[12,28,1024]{2,1,0:T(8,128)} %get-tuple-element.10.refs_1_, bf16[768,1024]{1,0:T(8,128)(2,1)} %get-tuple-element.11.refs_2_), custom_call_target="tpu_custom_call" | custom-call | tf_op jit(solution)/shard_map/pallas_call | solution.py:668

commit v4 on v3

--- a/solution.py
+++ b/solution.py
@@ -18,7 +18,8 @@
 NX, NY, NZ = 4, 4, 8
 MROW = 28
 CHUNKS, WIDE = 4, 256
-HALF = NARROW = WIDE // 2
+PARTS, HALF, NARROW = 6, 256, 128
+CHIPS = 32
 SLOTS = 4
 PIECES = 4
 SCALE = 0.2 * math.sqrt(max(F, D))
@@ -85,10 +86,15 @@
             out = jnp.where((lane >> 5) == turn, pltpu.roll(wide, 32 * turn, 1), out)
         return out[0:1]
 
-    same_row = ((r0 >> 2) & 3) == (r1 >> 5)
-    wanted = ((r0 >> 4) * SLOTS + (r0 & 3)).astype(F32)
-    forward = onehot(same_row & (tiled(code) == wanted))
-    forward_over = onehot(same_row & (tiled(code_over) == wanted))
+    f0, f1 = iota((512, 128), 0), iota((512, 128), 1)
+    same_row = ((f0 >> 2) & 3) == (f1 >> 5)
+    chip_at = (f0 >> 4).astype(F32)
+
+    def outward(row):
+        meant = same_row & (tiled(row) == chip_at)
+        return [onehot(meant & ((f0 & 3) == q)) for q in range(4)]
+
+    forward, forward_over = outward(code), outward(code_over)
     code_col = jnp.sum(
         jnp.where(r1 == (r0 & 31), jnp.broadcast_to(code, (128, 128)), 0.0), axis=1, keepdims=True
     )
@@ -121,15 +127,12 @@
     own,
     nest,
     zs_f,
-    zr_f,
     zs_o,
-    zr_o,
+    raw,
     zs_r,
     zr_r,
-    ys_p,
     x_in,
     x_d,
-    ys_o,
     x_a,
     x_b,
     gram_f,
@@ -146,11 +149,8 @@
     far_sem,
     comb_sem,
     z_send,
-    zf_sem,
-    zo_sem,
     r_send,
     zr_sem,
-    y_send,
     in_sem,
     all_in,
 ):
@@ -183,18 +183,20 @@
 
     def load(k):
         return pltpu.make_async_copy(
-            grads_hbm.at[:, :, pl.ds(k * WIDE, WIDE)], grads.at[k], load_sem.at[k]
+            grads_hbm.at[pl.ds(4 * (k % 3), 4), :, pl.ds(512 * (k // 3), 512)],
+            grads.at[k],
+            load_sem.at[k],
         )
 
-    load_momentum = pltpu.make_async_copy(momentum_hbm, momentum, load_sem.at[CHUNKS])
-    for k in range(CHUNKS):
+    load_momentum = pltpu.make_async_copy(momentum_hbm, momentum, load_sem.at[PARTS])
+    for k in range(PARTS):
         load(k).start()
     load_momentum.start()
 
-    def store(i, k):
+    def store(i, half):
         src, dst = ((newm_ref, newm_hbm), (update_ref, update_hbm))[i]
-        cols = pl.ds(k * WIDE, WIDE)
-        return pltpu.make_async_copy(src.at[:, :, cols], dst.at[:, :, cols], store_sem.at[i, k])
+        cols = pl.ds(512 * half, 512)
+        return pltpu.make_async_copy(src.at[:, :, cols], dst.at[:, :, cols], store_sem.at[i, half])
 
     store_owned = pltpu.make_async_copy(owned_ref, owned_hbm, store_sem.at[2, 0])
 
@@ -209,15 +211,16 @@
             barrier, 1, device_id=at(other // 2, z, other % 2), device_id_type=MESH
         )
 
-    owner = jnp.concatenate([owners_ref[...], jnp.zeros((1, 16), I32)], axis=1)
-    owner = pltpu.roll(jnp.broadcast_to(owner, (8, 128)), (128 - MROW * x) % 128, 1)
-    forward, forward_over, back, owns = routes(owner, z * SLOTS + y)
-    m_forward[...] = forward
-    m_over[...] = forward_over
-    for q in range(4):
-        m_back[128 * q : 128 * (q + 1)] = back[q]
-    m_owns[...] = jnp.broadcast_to(owns, (8, 128))
-    nest[...] = jnp.zeros_like(nest)
+    def make_tables():
+        owner = jnp.concatenate([owners_ref[...], jnp.zeros((1, 16), I32)], axis=1)
+        owner = pltpu.roll(jnp.broadcast_to(owner, (8, 128)), (128 - MROW * x) % 128, 1)
+        forward, forward_over, back, owns = routes(owner, z * SLOTS + y)
+        for q in range(4):
+            m_forward[:, 128 * q : 128 * (q + 1)] = forward[q]
+            m_over[:, 128 * q : 128 * (q + 1)] = forward_over[q]
+            m_back[128 * q : 128 * (q + 1)] = back[q]
+        m_owns[...] = jnp.broadcast_to(owns, (8, 128))
+        nest[...] = jnp.zeros_like(nest)
 
     p0, p1 = iota((112, 128), 0), iota((112, 128), 1)
     quarter = (
@@ -227,30 +230,27 @@
     def packing(parity):
         return onehot(p1 == p0 + 4 * quarter + 4 * parity)
 
-    def window(k, to, table, g):
+    def window(k, to, table):
         start = pl.multiple_of(((MROW * to) // 8) * 8, 8)
-        rows = grads[k, 4 * g : 4 * g + 4, pl.ds(start, 32), :].astype(BF).reshape(128, WIDE)
+        rows = grads[k, :, pl.ds(start, 32), :].astype(BF).reshape(128, 2 * HALF)
         return dot(table, rows)
 
     def pack(k):
         load(k).wait()
         odd = packing((x + 1) % 2)
         even = packing(x % 2)
-        for g in range(3):
-            v = window(k, far, even, g).astype(BF)
-            s_far[0, k, g] = v[:, :HALF]
-            s_far[1, k, g] = v[:, HALF:]
-            v = window(k, right, odd, g)
-            part[0, k, g] = v[:, :HALF]
-            s_direct[0, k, g] = v[:, HALF:].astype(BF)
-            v = window(k, left, odd, g)
-            part[1, k, g] = v[:, HALF:]
-            s_direct[1, k, g] = v[:, :HALF].astype(BF)
+        v = window(k, far, even).astype(BF)
+        s_far[0, k] = v[:, :HALF]
+        s_far[1, k] = v[:, HALF:]
+        v = window(k, right, odd)
+        part[0, k] = v[:, :HALF]
+        s_direct[0, k] = v[:, HALF:].astype(BF)
+        v = window(k, left, odd)
+        part[1, k] = v[:, HALF:]
+        s_direct[1, k] = v[:, :HALF].astype(BF)
 
     def pack_own(k):
-        even = packing(x % 2)
-        for g in range(3):
-            own[k, g] = window(k, x, even, g)
+        own[k] = window(k, x, packing(x % 2))
 
     towards = ((right, here), (left, here))
 
@@ -276,70 +276,72 @@
         for way in range(2):
             wait_recv(r_direct.at[way, k], direct_sem.at[way, k])
             wait_recv(r_comb.at[way, k], comb_sem.at[way, k])
-        low = own[k, :, :, :HALF] + r_direct[1, k].astype(F32) + r_comb[0, k].astype(F32)
-        high = own[k, :, :, HALF:] + r_direct[0, k].astype(F32) + r_comb[1, k].astype(F32)
-        own[k, :, :, :HALF] = low
-        own[k, :, :, HALF:] = high
-        for g in range(3):
-            for rr in range(4):
-                total = own[k, g, MROW * rr : MROW * (rr + 1), :]
-                cols = slice(k * WIDE, (k + 1) * WIDE)
-                moved = momentum_decay * momentum[4 * g + rr, :, cols] + total
-                newm_ref[4 * g + rr, :, cols] = moved
-                nest[g, 32 * rr : 32 * rr + MROW, :] = total + momentum_decay * moved
-        store(0, k).start()
-
-    def send_z(zs, zr, k, sem, recv_sem):
-        zr[k, pl.ds(z, 1)] = zs[k, pl.ds(z, 1)]
-        for step in (1, 7, 2, 6, 3, 5, 4):
-            to = (z + step) % NZ
-            send(zs.at[k, to], zr.at[k, z], sem, recv_sem.at[k], at(y, to, c))
-
-    def forward_z(k):
-        for g in range(3):
-            rows = nest[g].astype(BF)
-            zs_f[k, :, g] = dot(m_forward[...], rows).astype(BF).reshape(NZ, 16, WIDE)
-        send_z(zs_f, zr_f, k, z_send.at[0], zf_sem)
-        for g in range(3):
-            rows = nest[g].astype(BF)
-            zs_o[k, :, g] = dot(m_over[...], rows).astype(BF).reshape(NZ, 16, WIDE)
-
-    def forward_over_z(k):
-        send_z(zs_o, zr_o, k, z_send.at[1], zo_sem)
-
-    i0, i1 = iota((128, 128), 0), iota((128, 128), 1)
-    to_slots = lambda: onehot(i1 == ((i0 & 31) << 2) + (i0 >> 5))
-    from_slots = lambda: onehot(i0 == ((i1 & 31) << 2) + (i1 >> 5))
-
-    def others(n, me):
-        return [(me + step) % n for step in range(1, n)]
-
-    def relay(k, zr, ys, sem, core):
-        table = to_slots()
-        for g in range(3):
-            rows = zr[k, :, g].reshape(128, WIDE)
-            ys[k, :, g] = dot(table, rows).astype(BF).reshape(SLOTS, 32, WIDE)
-        for to in others(NY, y):
-            send(ys.at[k, to], x_in.at[k, e], y_send.at[sem], in_sem.at[k], at(to, z, core))
+        low = own[k, :, :HALF] + r_direct[1, k].astype(F32) + r_comb[0, k].astype(F32)
+        high = own[k, :, HALF:] + r_direct[0, k].astype(F32) + r_comb[1, k].astype(F32)
+        own[k, :, :HALF] = low
+        own[k, :, HALF:] = high
+        g, half = k % 3, k // 3
+        cols = slice(512 * half, 512 * (half + 1))
+        for rr in range(4):
+            total = own[k, MROW * rr : MROW * (rr + 1), :]
+            moved = momentum_decay * momentum[4 * g + rr, :, cols] + total
+            newm_ref[4 * g + rr, :, cols] = moved
+            nest[32 * rr : 32 * rr + MROW, :] = total + momentum_decay * moved
+        if g == 2:
+            store(0, half).start()
+
+    def send_out(k, zs, core, sem):
+        @pl.loop(0, CHIPS)
+        def _(i):
+            j = i // 4
+            to_z = (z + 4 + (1 - 2 * (j % 2)) * ((j + 1) // 2)) % NZ
+            to_y = (y + i) % NY
+
+            @pl.when(jnp.logical_or(i != 28, c != core))
+            def _():
+                send(
+                    zs.at[k, to_z * SLOTS + to_y], raw.at[k, here], sem, in_sem.at[k],
+                    at(to_y, to_z, core),
+                )
 
         @pl.when(c == core)
         def _():
-            x_in[k, pl.ds(e, 1)] = ys[k, pl.ds(y, 1)]
-
-        @pl.when(c != core)
-        def _():
-            send(ys.at[k, y], x_in.at[k, e], y_send.at[sem + 1], in_sem.at[k], at(y, z, core))
-
-    def relay_p(k):
-        wait_recv(zr_f.at[k, pl.ds(0, 7)], zf_sem.at[k])
-        relay(k, zr_f, ys_p, 0, 0)
-
-    def relay_o(k):
-        wait_recv(zr_o.at[k, pl.ds(0, 7)], zo_sem.at[k])
-        relay(k, zr_o, ys_o, 2, 1)
+            raw[k, pl.ds(here, 1)] = zs[k, pl.ds(z * SLOTS + y, 1)]
+
+    def rows_out(k):
+        rows = nest[...].astype(BF)
+        rows = jnp.concatenate([rows[:, NARROW * q : NARROW * (q + 1)] for q in range(4)], axis=0)
+        zs_f[k] = dot(m_forward[...], rows).astype(BF).reshape(CHIPS, 16, NARROW)
+        send_out(k, zs_f, 0, z_send.at[0])
+        zs_o[k] = dot(m_over[...], rows).astype(BF).reshape(CHIPS, 16, NARROW)
+
+    def rows_out_over(k):
+        send_out(k, zs_o, 1, z_send.at[1])
+
+    i0, i1 = iota((128, 128), 0), iota((128, 128), 1)
+    to_columns = lambda: onehot(i1 == ((i0 & 31) << 2) + (i0 >> 5))
+    from_columns = lambda: onehot(i0 == ((i1 & 31) << 2) + (i1 >> 5))
+
+    def rows_in(k):
+        wait_recv(raw.at[k, pl.ds(0, 63)], in_sem.at[k])
+        g, half = k % 3, k // 3
+        rows = jnp.concatenate(
+            [raw[k, 8 * i : 8 * (i + 1)].reshape(128, NARROW) for i in range(8)], axis=1
+        )
+        rows = dot(to_columns(), rows).astype(BF)
+        for q in range(4):
+            for i in range(8):
+                first = 256 * g + 32 * i
+                x_in[
+                    2 * half + q // 2, first : first + 32,
+                    NARROW * (q % 2) : NARROW * (q % 2 + 1),
+                ] = rows[32 * q : 32 * (q + 1), NARROW * i : NARROW * (i + 1)]
+        if g == 2:
+            add_gram(x_in, 2 * half)
+            add_gram(x_in, 2 * half + 1)
 
     def matrix(ref, k):
-        return ref[k].reshape(F, WIDE)
+        return ref[k]
 
     blocks = [(i, j) for i in range(3) for j in range(i, 3)]
 
@@ -383,7 +385,7 @@
     def advance(src, dst, k):
         rows = matrix(src, k)
         out = coeff_first * rows.astype(F32) + dot(poly_b[...], rows)
-        dst[k] = out.astype(BF).reshape(8, 3, 32, WIDE)
+        dst[k] = out.astype(BF)
 
     def finish(src, dst, done, between):
         d0, d1 = iota((256, 256), 0), iota((256, 256), 1)
@@ -409,16 +411,20 @@
         if k % 2 == 0:
             return
         half = k // 2
-        table = from_slots()
+        table = from_columns()
 
         @pl.loop(0, 8)
         def _(step):
-            to = (e + step) % 8
+            group = (here // 8 + step) % 8
             rows = jnp.concatenate(
                 [
                     jnp.concatenate(
                         [
-                            x_d[k - 1 + q // 2, to, g, :, NARROW * (q % 2) : NARROW * (q % 2 + 1)]
+                            x_d[
+                                k - 1 + q // 2,
+                                pl.ds(pl.multiple_of(256 * g + 32 * group, 32), 32),
+                                NARROW * (q % 2) : NARROW * (q % 2 + 1),
+                            ]
                             for g in range(3)
                         ],
                         axis=1,
@@ -427,47 +433,37 @@
                 ],
                 axis=0,
             )
-            rows = dot(table, rows).astype(BF).reshape(NZ, 16, 3 * NARROW)
-            zs_r[half, pl.ds(to * NZ, NZ)] = rows
-
-            for near in (0, 1, 7, 2, 6, 3, 5, 4):
-                to_z = (z + near) % NZ
-
-                def give():
+            rows = dot(table, rows).astype(BF).reshape(8, 16, 3 * NARROW)
+            zs_r[half, pl.ds(group * 8, 8)] = rows
+
+            @pl.loop(0, 8)
+            def _(i):
+                to = group * 8 + i
+
+                @pl.when(to != here)
+                def _():
                     send(
-                        zs_r.at[half, to * NZ + to_z], zr_r.at[half, z * SLOTS + y], r_send,
-                        zr_sem.at[half], at(to // 2, to_z, to % 2),
+                        zs_r.at[half, to], zr_r.at[half, z * SLOTS + y], r_send, zr_sem.at[half],
+                        (x, to),
                     )
 
-                if near == 0:
-
-                    @pl.when(step > 0)
-                    def _():
-                        give()
-                else:
-                    give()
-
-        zr_r[half, pl.ds(z * SLOTS + y, 1)] = zs_r[half, pl.ds(e * NZ + z, 1)]
-
-    def gram_in(k):
-        wait_recv(x_in.at[k, pl.ds(0, 7)], in_sem.at[k])
-        add_gram(x_in, k)
-
-    def primary_gram(k):
+        zr_r[half, pl.ds(z * SLOTS + y, 1)] = zs_r[half, pl.ds(here, 1)]
+
+    def primary_in(k):
         @pl.when(c == 0)
         def _():
-            gram_in(k)
+            rows_in(k)
 
     def put_owned():
         t0, t1 = iota((192, 192), 0), iota((192, 192), 1)
-        g0 = jnp.where((t1 % 96) >= 64, 2, jnp.where((t1 % 96) >= 32, 1, 0))
-        c0 = jnp.where(t1 >= 96, 1, 0)
-        place = ((t1 >> 2) & 7) * 24 + c0 * 12 + g0 * 4 + (t1 & 3)
+        place = ((t1 & 63) >> 2) * 12 + (t1 >> 6) * 4 + (t1 & 3)
         kept = (m_owns[0:1, 0:1] > 0.5) | (c == 1)
         table = onehot((t0 == place) & kept)
         for k in range(CHUNKS):
             for b in range(4):
-                rows = x_d[k, 2 * b : 2 * b + 2].reshape(192, WIDE)
+                rows = jnp.concatenate(
+                    [x_d[k, 256 * g + 64 * b : 256 * g + 64 * (b + 1)] for g in range(3)], axis=0
+                )
                 owned_ref[192 * b : 192 * (b + 1), k * WIDE : (k + 1) * WIDE] = dot(
                     table, rows
                 ).astype(BF)
@@ -491,8 +487,7 @@
                     update_ref[4 * g + rr, :, first : first + NARROW] = rows[
                         32 * rr : 32 * rr + MROW, NARROW * g : NARROW * (g + 1)
                     ]
-        for k in (2 * half, 2 * half + 1):
-            store(1, k).start()
+        store(1, half).start()
 
     pack(0)
     pl.semaphore_wait(barrier, 16)
@@ -505,72 +500,63 @@
     pack(2)
     send_first(2)
     pack_own(0)
+    make_tables()
     load_momentum.wait()
-    for k in range(CHUNKS):
-        if k + 1 < CHUNKS:
+    for k in range(PARTS):
+        if k + 1 < PARTS:
             send_combined(k + 1)
-        if k + 3 < CHUNKS:
+        if k + 3 < PARTS:
             pack(k + 3)
             send_first(k + 3)
-        if k + 1 < CHUNKS:
+        if k + 1 < PARTS:
             pack_own(k + 1)
         gradient(k)
-        forward_z(k)
-        if k >= 1:
-            relay_p(k - 1)
+        if k == 0:
+            pl.semaphore_wait(all_in, NZ - 1)
+        rows_out(k)
         if k >= 2:
-            primary_gram(k - 2)
-    forward_over_z(0)
-    forward_over_z(1)
-    relay_p(CHUNKS - 1)
-    forward_over_z(2)
-    forward_over_z(3)
-    primary_gram(CHUNKS - 2)
-    primary_gram(CHUNKS - 1)
-    pl.semaphore_wait(all_in, NZ - 1)
+            primary_in(k - 2)
+    rows_out_over(0)
+    rows_out_over(1)
+    primary_in(PARTS - 2)
+    rows_out_over(2)
+    rows_out_over(3)
+    rows_out_over(4)
+    rows_out_over(5)
 
     @pl.when(c == 0)
     def _():
-        def between():
-            relay_o(0)
-            relay_o(1)
-
-        finish(x_in, x_d, send_back, between)
-        relay_o(2)
-        relay_o(3)
+        rows_in(PARTS - 1)
+        finish(x_in, x_d, send_back, lambda: None)
 
     @pl.when(c == 1)
     def _():
-        for k in range(CHUNKS):
-            relay_o(k)
-        for k in range(CHUNKS):
-            gram_in(k)
+        for k in range(PARTS):
+            rows_in(k)
         finish(x_in, x_d, lambda k: None, lambda: None)
 
     put_owned()
     for half in range(2):
         unpack(half)
-    for k in range(CHUNKS):
-        store(0, k).wait()
-        store(1, k).wait()
+    for half in range(2):
+        store(0, half).wait()
+        store(1, half).wait()
     store_owned.wait()
 
     wait_send(s_far, x_send.at[0])
     wait_send(s_direct, x_send.at[1])
     wait_send(s_comb, x_send.at[2])
-    for i, ref in enumerate((zs_f, zs_o)):
-        wait_send(ref.at[:, pl.ds(0, 7)], z_send.at[i])
-    wait_send(ys_p.at[:, pl.ds(0, 3)], y_send.at[0])
-    wait_send(ys_o.at[:, pl.ds(0, 3)], y_send.at[2])
+
+    @pl.when(c == 0)
+    def _():
+        wait_send(zs_f.at[:, pl.ds(0, CHIPS - 1)], z_send.at[0])
+        wait_send(zs_o, z_send.at[1])
+        wait_send(zs_r.at[:, pl.ds(0, 63)], r_send)
 
     @pl.when(c == 1)
     def _():
-        wait_send(ys_p.at[:, 0], y_send.at[1])
-
-    @pl.when(c == 0)
-    def _():
-        wait_send(ys_o.at[:, 0], y_send.at[3])
-        wait_send(zs_r.at[:, pl.ds(0, 63)], r_send)
+        wait_send(zs_f, z_send.at[0])
+        wait_send(zs_o.at[:, pl.ds(0, CHIPS - 1)], z_send.at[1])
 
 
 def scratch():
@@ -578,49 +564,44 @@
         return pltpu.VMEM(shape, dtype)
 
     dma = pltpu.SemaphoreType.DMA
-    x_half = (2, CHUNKS, 3, 112, HALF)
-    z_all = (CHUNKS, NZ, 3, 16, WIDE)
-    plane = (CHUNKS, 8, 3, 32, WIDE)
-    quarter = (CHUNKS, SLOTS, 3, 32, WIDE)
+    x_half = (2, PARTS, 112, HALF)
+    whole = (CHUNKS, F, WIDE)
     return [
         vmem(12, MROW, D, dtype=F32),
         vmem(12, MROW, D, dtype=F32),
         vmem(F, D),
-        vmem(CHUNKS, 12, 112, WIDE, dtype=F32),
+        vmem(PARTS, 4, 112, 512, dtype=F32),
         vmem(12, MROW, D, dtype=F32),
         *[vmem(*x_half) for _ in range(6)],
         vmem(*x_half, dtype=F32),
-        vmem(CHUNKS, 3, 112, WIDE, dtype=F32),
-        vmem(3, 128, WIDE, dtype=F32),
-        *[vmem(*z_all) for _ in range(4)],
+        vmem(PARTS, 112, 512, dtype=F32),
+        vmem(128, 512, dtype=F32),
+        vmem(PARTS, CHIPS, 16, NARROW),
+        vmem(PARTS, CHIPS, 16, NARROW),
+        vmem(PARTS, 64, 16, NARROW),
         vmem(2, 64, 16, 3 * NARROW),
-        vmem(2, 32, 16, 3 * NARROW),
-        vmem(*quarter),
-        vmem(*plane),
-        vmem(*plane),
-        vmem(*quarter),
-        vmem(*plane),
-        vmem(*plane),
+        vmem(2, CHIPS, 16, 3 * NARROW),
+        vmem(*whole),
+        vmem(*whole),
+        vmem(*whole),
+        vmem(*whole),
         vmem(F, F, dtype=F32),
         vmem(F, F),
         vmem(F, F),
-        vmem(128, 128),
-        vmem(128, 128),
+        vmem(512, 512),
+        vmem(512, 512),
         vmem(512, 512),
         vmem(8, 128, dtype=F32),
-        dma((CHUNKS + 1,)),
-        dma((3, CHUNKS)),
+        dma((PARTS + 1,)),
+        dma((3, 2)),
         dma((3,)),
-        dma((2, CHUNKS)),
-        dma((2, CHUNKS)),
-        dma((2, CHUNKS)),
+        dma((2, PARTS)),
+        dma((2, PARTS)),
+        dma((2, PARTS)),
         dma((2,)),
-        dma((CHUNKS,)),
-        dma((CHUNKS,)),
         dma(()),
         dma((2,)),
-        dma((4,)),
-        dma((CHUNKS,)),
+        dma((PARTS,)),
         pltpu.SemaphoreType.REGULAR,
     ]
 

time: 86.8 us -> 84.2 us (0.970)
  Pallas kernels: 85.9 us -> 83.3 us
    pallas_call x1, Pallas kernels: 81.6 us -> 79 us  [local(): pl.pallas_call(kernel, out_shape=outs, in_specs=[anywhere, anywhere, vmem...]
where the time goes in v4:
time: 84.2 us; the launch traced here: 84.1 us
  Pallas kernels  83.3 us (99%)
    pallas_call x1, Pallas kernels, local(): pl.pallas_call(kernel, out_shape=outs, in_specs=[anywhere, anywhere, vmem...  79 us
    pallas_call x1, Pallas kernels, local(): pl.pallas_call(hand_over, out_shape=outs, in_specs=[anywhere] * 3, out_sp...  4.27 us

profile of v4, /device:TPU:1, one launch (start us, length us, event | category | flops | bytes accessed | tf_op | source)
XLA Modules:
  0.0 84.1 jit_solution(10063216892209154200)
XLA Ops:
  0.6 79.0 %shard_map.58 = (f32[12,28,1024]{2,1,0:T(8,128)}, f32[12,28,1024]{2,1,0:T(8,128)}, bf16[768,1024]{1,0:T(8,128)(2,1)}) custom-call(f32[12,112,1024]{2,1,0:T(8,128)} %bitcast.8, f32[12,28,1024]{2,1,0:T(8,128)} %bitcast.9, s32[1,112]{1,0:T(1,128)} %bitcast.10), custom_call_target="tpu_custom_call" | custom-call | tf_op jit(solution)/shard_map/pallas_call | solution.py:639
  79.6 4.3 %shard_map.59 = (f32[12,28,1024]{2,1,0:T(8,128)}, f32[12,28,1024]{2,1,0:T(8,128)}, bf16[768,1024]{1,0:T(8,128)(2,1)}) custom-call(f32[12,28,1024]{2,1,0:T(8,128)} %get-tuple-element.9.refs_0_, f32[12,28,1024]{2,1,0:T(8,128)} %get-tuple-element.10.refs_1_, bf16[768,1024]{1,0:T(8,128)(2,1)} %get-tuple-element.11.refs_2_), custom_call_target="tpu_custom_call" | custom-call | tf_op jit(solution)/shard_map/pallas_call | solution.py:649

commit v5 on v4

--- a/solution.py
+++ b/solution.py
@@ -22,6 +22,7 @@
 CHIPS = 32
 SLOTS = 4
 PIECES = 4
+LIMIT = 48
 SCALE = 0.2 * math.sqrt(max(F, D))
 
 momentum_decay = 0.95
@@ -109,9 +110,6 @@
     grads_hbm,
     momentum_hbm,
     owners_ref,
-    newm_hbm,
-    update_hbm,
-    owned_hbm,
     newm_ref,
     update_ref,
     owned_ref,
@@ -133,7 +131,6 @@
     zr_r,
     x_in,
     x_d,
-    x_a,
     x_b,
     gram_f,
     gram_b,
@@ -143,7 +140,6 @@
     m_back,
     m_owns,
     load_sem,
-    store_sem,
     x_send,
     direct_sem,
     far_sem,
@@ -193,13 +189,6 @@
         load(k).start()
     load_momentum.start()
 
-    def store(i, half):
-        src, dst = ((newm_ref, newm_hbm), (update_ref, update_hbm))[i]
-        cols = pl.ds(512 * half, 512)
-        return pltpu.make_async_copy(src.at[:, :, cols], dst.at[:, :, cols], store_sem.at[i, half])
-
-    store_owned = pltpu.make_async_copy(owned_ref, owned_hbm, store_sem.at[2, 0])
-
     barrier = pltpu.get_barrier_semaphore()
     for device in ((right, here), (left, here)):
         pl.semaphore_signal(barrier, 1, device_id=device, device_id_type=MESH)
@@ -287,8 +276,6 @@
             moved = momentum_decay * momentum[4 * g + rr, :, cols] + total
             newm_ref[4 * g + rr, :, cols] = moved
             nest[32 * rr : 32 * rr + MROW, :] = total + momentum_decay * moved
-        if g == 2:
-            store(0, half).start()
 
     def send_out(k, zs, core, sem):
         @pl.loop(0, CHIPS)
@@ -382,9 +369,11 @@
             if i != j:
                 block(poly_b, j, i)[...] = value.T
 
-    def advance(src, dst, k):
+    def advance(src, dst, k, scale=None):
         rows = matrix(src, k)
         out = coeff_first * rows.astype(F32) + dot(poly_b[...], rows)
+        if scale is not None:
+            out = out * scale
         dst[k] = out.astype(BF)
 
     def finish(src, dst, done, between):
@@ -395,11 +384,9 @@
         inverse = 1.0 / (jnp.sqrt(squares) + epsilon_norm)
         for i, j in blocks:
             put_gram(i, j, block(gram_f, i, j)[...] * (inverse * inverse))
-        for k in range(CHUNKS):
-            x_a[k] = (src[k].astype(F32) * inverse).astype(BF)
         poly()
         for k in range(CHUNKS):
-            advance(x_a, x_b, k)
+            advance(src, x_b, k, inverse)
         between()
         whole_gram(x_b)
         poly()
@@ -467,7 +454,6 @@
                 owned_ref[192 * b : 192 * (b + 1), k * WIDE : (k + 1) * WIDE] = dot(
                     table, rows
                 ).astype(BF)
-        store_owned.start()
 
     def unpack(half):
         @pl.when(c == 0)
@@ -487,7 +473,6 @@
                     update_ref[4 * g + rr, :, first : first + NARROW] = rows[
                         32 * rr : 32 * rr + MROW, NARROW * g : NARROW * (g + 1)
                     ]
-        store(1, half).start()
 
     pack(0)
     pl.semaphore_wait(barrier, 16)
@@ -538,10 +523,6 @@
     put_owned()
     for half in range(2):
         unpack(half)
-    for half in range(2):
-        store(0, half).wait()
-        store(1, half).wait()
-    store_owned.wait()
 
     wait_send(s_far, x_send.at[0])
     wait_send(s_direct, x_send.at[1])
@@ -567,9 +548,6 @@
     x_half = (2, PARTS, 112, HALF)
     whole = (CHUNKS, F, WIDE)
     return [
-        vmem(12, MROW, D, dtype=F32),
-        vmem(12, MROW, D, dtype=F32),
-        vmem(F, D),
         vmem(PARTS, 4, 112, 512, dtype=F32),
         vmem(12, MROW, D, dtype=F32),
         *[vmem(*x_half) for _ in range(6)],
@@ -584,7 +562,6 @@
         vmem(*whole),
         vmem(*whole),
         vmem(*whole),
-        vmem(*whole),
         vmem(F, F, dtype=F32),
         vmem(F, F),
         vmem(F, F),
@@ -593,7 +570,6 @@
         vmem(512, 512),
         vmem(8, 128, dtype=F32),
         dma((PARTS + 1,)),
-        dma((3, 2)),
         dma((3,)),
         dma((2, PARTS)),
         dma((2, PARTS)),
@@ -607,22 +583,17 @@
 
 
 def hand_over(*refs):
-    srcs, dsts, held = refs[:3], refs[3:6], refs[6:9]
-    in_sem, out_sem = refs[9:]
-
-    def move(i, piece, src, dst, sem):
+    srcs, dsts, sem = refs[:3], refs[3:6], refs[6]
+    moves = []
+    for i, (src, dst) in enumerate(zip(srcs, dsts)):
         rows = src.shape[0] // PIECES
-        part = pl.ds(piece * rows, rows)
-        return pltpu.make_async_copy(src.at[part], dst.at[part], sem.at[i, piece])
-
-    each = [(i, piece) for i in range(3) for piece in range(PIECES)]
-    for i, piece in each:
-        move(i, piece, srcs[i], held[i], in_sem).start()
-    for i, piece in each:
-        move(i, piece, srcs[i], held[i], in_sem).wait()
-        move(i, piece, held[i], dsts[i], out_sem).start()
-    for i, piece in each:
-        move(i, piece, held[i], dsts[i], out_sem).wait()
+        for piece in range(PIECES):
+            part = pl.ds(piece * rows, rows)
+            moves.append(pltpu.make_async_copy(src.at[part], dst.at[part], sem.at[i, piece]))
+    for move in moves:
+        move.start()
+    for move in moves:
+        move.wait()
 
 
 def local(partial_grads, momentum, owners):
@@ -640,20 +611,19 @@
         kernel,
         out_shape=outs,
         in_specs=[anywhere, anywhere, vmem],
-        out_specs=(anywhere,) * 3,
+        out_specs=(vmem,) * 3,
         scratch_shapes=scratch(),
         compiler_params=pltpu.CompilerParams(
-            collective_id=0, has_side_effects=True, vmem_limit_bytes=60 << 20
+            collective_id=0, has_side_effects=True, vmem_limit_bytes=LIMIT << 20
         ),
     )(grads, held, owners)
     new_momentum, update, owned = pl.pallas_call(
         hand_over,
         out_shape=outs,
-        in_specs=[anywhere] * 3,
+        in_specs=[vmem] * 3,
         out_specs=(anywhere,) * 3,
-        scratch_shapes=[pltpu.VMEM(out.shape, out.dtype) for out in outs]
-        + [pltpu.SemaphoreType.DMA((3, PIECES))] * 2,
-        compiler_params=pltpu.CompilerParams(vmem_limit_bytes=60 << 20),
+        scratch_shapes=[pltpu.SemaphoreType.DMA((3, PIECES))],
+        compiler_params=pltpu.CompilerParams(vmem_limit_bytes=8 << 20),
     )(*results)
     return (
         jnp.transpose(new_momentum, (1, 0, 2)),

time: 84.2 us -> 81.1 us (0.963)
  Pallas kernels: 83.3 us -> 79.5 us
    pallas_call x1, Pallas kernels: 4.27 us -> 2.28 us  [local(): pl.pallas_call(hand_over, out_shape=outs, in_specs=[vmem] * 3, out_specs=...]
    pallas_call x1, Pallas kernels: 79 us -> 77.2 us  [local(): pl.pallas_call(kernel, out_shape=outs, in_specs=[anywhere, anywhere, vmem...]
where the time goes in v5:
time: 81.1 us; the launch traced here: 81 us
  Pallas kernels  79.5 us (98%)
    pallas_call x1, Pallas kernels, local(): pl.pallas_call(kernel, out_shape=outs, in_specs=[anywhere, anywhere, vmem...  77.2 us
    pallas_call x1, Pallas kernels, local(): pl.pallas_call(hand_over, out_shape=outs, in_specs=[vmem] * 3, out_specs=...  2.28 us

profile of v5, /device:TPU:1, one launch (start us, length us, event | category | flops | bytes accessed | tf_op | source)
XLA Modules:
  0.0 81.0 jit_solution(1617567504689974624)
XLA Ops:
  0.6 0.0 copy-start
  0.6 0.6 copy-done
  1.3 77.2 %shard_map.58 = (f32[12,28,1024]{2,1,0:T(8,128)S(1)}, f32[12,28,1024]{2,1,0:T(8,128)S(1)}, bf16[768,1024]{1,0:T(8,128)(2,1)S(1)}) custom-call(f32[12,112,1024]{2,1,0:T(8,128)} %bitcast.9, f32[12,28,1024]{2,1,0:T(8,128)} %bitcast.10, s32[1,112]{1,0:T(1,128)S(1)} %bitcast.8), custom_call_target="tpu_custom_call" | custom-call | tf_op jit(solution)/shard_map/pallas_call | solution.py:610
  78.5 2.3 %shard_map.59 = (f32[12,28,1024]{2,1,0:T(8,128)}, f32[12,28,1024]{2,1,0:T(8,128)}, bf16[768,1024]{1,0:T(8,128)(2,1)}) custom-call(f32[12,28,1024]{2,1,0:T(8,128)S(1)} %get-tuple-element.9.refs_0_, f32[12,28,1024]{2,1,0:T(8,128)S(1)} %get-tuple-element.10.refs_1_, bf16[768,1024]{1,0:T(8,128)(2,1)S(1)} %get-tuple-element.11.refs_2_), custom_call_target="tpu_custom_call" | custom-call | tf_op jit(solution)/shard_map/pallas_call | solution.py:620
Async XLA Ops:
  0.6 0.7 copy-start

commit v6 on v5

--- a/solution.py
+++ b/solution.py
@@ -324,8 +324,7 @@
                     NARROW * (q % 2) : NARROW * (q % 2 + 1),
                 ] = rows[32 * q : 32 * (q + 1), NARROW * i : NARROW * (i + 1)]
         if g == 2:
-            add_gram(x_in, 2 * half)
-            add_gram(x_in, 2 * half + 1)
+            add_gram(x_in, half)
 
     def matrix(ref, k):
         return ref[k]
@@ -335,12 +334,14 @@
     def block(ref, i, j):
         return ref.at[256 * i : 256 * (i + 1), 256 * j : 256 * (j + 1)]
 
-    def add_gram(src, k):
-        rows = matrix(src, k)
+    def add_gram(src, half):
         for i, j in blocks:
-            new = dot_t(rows[256 * i : 256 * (i + 1)], rows[256 * j : 256 * (j + 1)])
+            new = 0.0
+            for k in (2 * half, 2 * half + 1):
+                rows = matrix(src, k)
+                new = new + dot_t(rows[256 * i : 256 * (i + 1)], rows[256 * j : 256 * (j + 1)])
             into = block(gram_f, i, j)
-            into[...] = new if k == 0 else into[...] + new
+            into[...] = new if half == 0 else into[...] + new
 
     def put_gram(i, j, value):
         value = value.astype(BF)
@@ -499,12 +500,12 @@
         if k == 0:
             pl.semaphore_wait(all_in, NZ - 1)
         rows_out(k)
+        if k == 0 or k == 2:
+            rows_out_over(k // 2)
         if k >= 2:
             primary_in(k - 2)
-    rows_out_over(0)
-    rows_out_over(1)
+    rows_out_over(2)
     primary_in(PARTS - 2)
-    rows_out_over(2)
     rows_out_over(3)
     rows_out_over(4)
     rows_out_over(5)

time: 81.1 us -> 78.2 us (0.964)
  Pallas kernels: 79.5 us -> 76.7 us
    pallas_call x1, Pallas kernels: 77.2 us -> 74.4 us  [local(): pl.pallas_call(kernel, out_shape=outs, in_specs=[anywhere, anywhere, vmem...]
where the time goes in v6:
time: 78.2 us; the launch traced here: 78.1 us
  Pallas kernels  76.7 us (98%)
  between operations  0.81 us (1%)
    pallas_call x1, Pallas kernels, local(): pl.pallas_call(kernel, out_shape=outs, in_specs=[anywhere, anywhere, vmem...  74.4 us
    pallas_call x1, Pallas kernels, local(): pl.pallas_call(hand_over, out_shape=outs, in_specs=[vmem] * 3, out_specs=...  2.28 us

profile of v6, /device:TPU:1, one launch (start us, length us, event | category | flops | bytes accessed | tf_op | source)
XLA Modules:
  0.0 78.1 jit_solution(7945585471785920154)
XLA Ops:
  0.6 0.0 copy-start
  0.6 0.6 copy-done
  1.3 74.4 %shard_map.58 = (f32[12,28,1024]{2,1,0:T(8,128)S(1)}, f32[12,28,1024]{2,1,0:T(8,128)S(1)}, bf16[768,1024]{1,0:T(8,128)(2,1)S(1)}) custom-call(f32[12,112,1024]{2,1,0:T(8,128)} %bitcast.9, f32[12,28,1024]{2,1,0:T(8,128)} %bitcast.10, s32[1,112]{1,0:T(1,128)S(1)} %bitcast.8), custom_call_target="tpu_custom_call" | custom-call | tf_op jit(solution)/shard_map/pallas_call | solution.py:611
  75.7 2.3 %shard_map.59 = (f32[12,28,1024]{2,1,0:T(8,128)}, f32[12,28,1024]{2,1,0:T(8,128)}, bf16[768,1024]{1,0:T(8,128)(2,1)}) custom-call(f32[12,28,1024]{2,1,0:T(8,128)S(1)} %get-tuple-element.9.refs_0_, f32[12,28,1024]{2,1,0:T(8,128)S(1)} %get-tuple-element.10.refs_1_, bf16[768,1024]{1,0:T(8,128)(2,1)S(1)} %get-tuple-element.11.refs_2_), custom_call_target="tpu_custom_call" | custom-call | tf_op jit(solution)/shard_map/pallas_call | solution.py:621
Async XLA Ops:
  0.6 0.7 copy-start
